TPU v7x, 32 devices: a whole 2x2x4 slice. The times are simulated.
32 devices in a mesh: groups: 2 (over x), lon: 16 (over z, y, core).
Axes of the slice: x: 2, y: 2, z: 4, core: 2. Of those that a mesh axis runs over, the one named last changes fastest.
Arguments:
- atmosphere: bfloat16 [16, 512, 1024], P('groups', 'lon'), parts along dimension 0, may hold values from -6 to 6
- cotangent: bfloat16 [16, 512, 1024], P('groups', 'lon'), parts along dimension 0, may hold values from -6 to 6
- ocean_state: bfloat16 [16, 512, 512], P('groups', 'lon'), parts along dimension 0, may hold values from -6 to 6
- ocean_mask: int32 [16, 512], P('groups', 'lon'), parts along dimension 0, may hold values 0 or 1
- projection: bfloat16 [1024, 3072], P('lon'), may hold values from -9 to 9
- output_weight: bfloat16 [1024, 1024], P('lon'), may hold values from -0.1875 to 0.1875
- attention_gain: float32 [1024], replicated, may hold values from 0.5 to 1.5
- surface_embed: float32 [1024], replicated, may hold values from -3 to 3
- surface_read: bfloat16 [512], replicated, may hold values from -0.25 to 0.25
- flux_weight: bfloat16 [1024, 4], replicated, may hold values from -0.1875 to 0.1875
- flux_embed: float32 [4, 512], replicated, may hold values from -3 to 3
- depthwise: float32 [7, 7, 512], replicated, may hold values from -0.875 to 0.875
- ocean_gain: float32 [512], replicated, may hold values from 0.5 to 1.5
- expand: bfloat16 [512, 2048], replicated, may hold values from -0.25 to 0.25
- contract: bfloat16 [2048, 512], replicated, may hold values from -0.125 to 0.125
- regrid_blocks: bfloat16 [16, 2, 256, 256], P('lon'), may hold values from -0.375 to 0.375
- regrid_target: int32 [16, 2], replicated, may hold values from 0 to 15, as said below
Outputs:
- atmosphere_out: bfloat16 [16, 512, 1024], P('groups', 'lon'), parts along dimension 0
- ocean_next: bfloat16 [16, 512, 512], P('groups', 'lon'), parts along dimension 0
- weight_grad: float32 [2048, 4096], P(('groups', 'lon')), parts along dimension 0
There are 2 independent parts, one for each index of `groups`. A program takes and returns all parts, laid end to end along the dimension named above; an argument that names none is the same for every part. Nothing has to cross between parts.
Inputs may be any that keep to these rules, and one draw needn't show every extreme that they name: `regrid_target`: column 0 names every ocean tile exactly once.
All inputs are finite; a program needn't handle non-finite values. No bound on the sum of `ocean_mask` on one device may be relied on, other than what follows from the above.
Results may differ from a plain program's by a relative error of at most 0.008.
The roundings to bfloat16 on the way count: a program that leaves them out, or rounds other values in their place, can miss the bound.
Values may be sent and summed in bfloat16 or wider, within the bound.
A program may use at most 128 MiB of HBM per device.

v0:
```python
import jax
import jax.numpy as jnp
from jax import lax
from jax.sharding import PartitionSpec as P

HEAD_DIM = 32
WIN = 8
KERNEL = 7


EPSILON = 1e-05
HIGHEST = lax.Precision.HIGHEST


def from_behind(block, axis, distance):
    devices = range(lax.axis_size(axis))
    route = [((i - distance) % len(devices), i) for i in devices]
    return lax.ppermute(block, axis, route)


def extended(shard, sides, width):
    for axis, dim in sides:
        peers, length = (lax.axis_size(axis), shard.shape[dim])
        up = [(i, (i + 1) % peers) for i in range(peers)]
        down = [(j, i) for i, j in up]
        last = lax.slice_in_dim(shard, length - width, length, axis=dim)
        leading = lax.slice_in_dim(shard, 0, width, axis=dim)
        before = lax.ppermute(last, axis, up)
        after = lax.ppermute(leading, axis, down)
        shard = jnp.concatenate([before, shard, after], axis=dim)
    return shard


def layer_norm(values, gain):
    center = values - jnp.mean(values, axis=-1, keepdims=True)
    spread = jnp.mean(center * center, axis=-1, keepdims=True)
    return center * lax.rsqrt(spread + EPSILON) * gain


def to_windows(values, window):
    height, width, depth = values.shape
    blocks = values.reshape(height // window, window, width // window, window, depth)
    return blocks.transpose(0, 2, 1, 3, 4).reshape(-1, window * window, depth)


def from_windows(values, height, width, window):
    depth = values.shape[-1]
    blocks = values.reshape(height // window, width // window, window, window, depth)
    return blocks.transpose(0, 2, 1, 3, 4).reshape(height, width, depth)


def split_three(packed, heads, head_size):
    windows, tokens = (packed.shape[0], packed.shape[1])
    width = heads * head_size
    query = packed[..., :width].reshape(windows, tokens, heads, head_size)
    keys = packed[..., width : 2 * width].reshape(windows, tokens, heads, head_size)
    values = packed[..., 2 * width :].reshape(windows, tokens, heads, head_size)
    return (query, keys, values)


def attend_forward(packed, heads, head_size):
    query, keys, values = split_three(packed, heads, head_size)
    scores = jnp.einsum(
        "wqhd,wkhd->whqk", query, keys, preferred_element_type=jnp.float32
    ) * head_size ** (-0.5)
    probs = jax.nn.softmax(scores, axis=-1)
    weights = probs.astype(jnp.bfloat16)
    mixed = jnp.einsum("whqk,wkhd->wqhd", weights, values, preferred_element_type=jnp.float32)
    return (
        mixed.reshape(packed.shape[0], packed.shape[1], heads * head_size).astype(jnp.bfloat16),
        probs,
        weights,
    )


def attend_backward(packed, probs, weights, grad_att, heads, head_size):
    query, keys, values = split_three(packed, heads, head_size)
    windows, tokens = (packed.shape[0], packed.shape[1])
    grad_heads = grad_att.reshape(windows, tokens, heads, head_size)
    grad_probs = jnp.einsum(
        "wqhd,wkhd->whqk", grad_heads, values, preferred_element_type=jnp.float32
    )
    grad_values = jnp.einsum(
        "whqk,wqhd->wkhd", weights, grad_heads, preferred_element_type=jnp.float32
    )
    inner = jnp.sum(grad_probs * probs, axis=-1, keepdims=True)
    grad_scores = (probs * (grad_probs - inner) * head_size ** (-0.5)).astype(jnp.bfloat16)
    grad_query = jnp.einsum(
        "whqk,wkhd->wqhd", grad_scores, keys, preferred_element_type=jnp.float32
    )
    grad_keys = jnp.einsum(
        "whqk,wqhd->wkhd", grad_scores, query, preferred_element_type=jnp.float32
    )
    width = heads * head_size
    joined = jnp.concatenate(
        [
            grad_query.reshape(windows, tokens, width),
            grad_keys.reshape(windows, tokens, width),
            grad_values.reshape(windows, tokens, width),
        ],
        axis=-1,
    )
    return joined.astype(jnp.bfloat16)


def depthwise_conv(padded, kernel, height, width):
    reach = kernel.shape[0]
    total = jnp.zeros((height, width, kernel.shape[2]), jnp.float32)
    for row in range(reach):
        for column in range(reach):
            total = (
                total + padded[row : row + height, column : column + width] * kernel[row, column]
            )
    return total


def transposed_product(left, right):
    return lax.dot_general(
        left, right, (((0,), (0,)), ((), ())), preferred_element_type=jnp.float32
    )


def per_device(
    atmosphere,
    cotangent,
    ocean_state,
    ocean_mask,
    projection,
    output_weight,
    attention_gain,
    surface_embed,
    surface_read,
    flux_weight,
    flux_embed,
    depthwise,
    ocean_gain,
    expand,
    contract,
    regrid_blocks,
    regrid_target,
):
    height, width, model = atmosphere.shape
    channels = ocean_state.shape[2]
    shift = WIN // 2
    tokens = height * width
    heads = model // HEAD_DIM
    devices = lax.axis_size("lon")
    position = lax.axis_index("lon")
    blocks = regrid_blocks[0]
    targets = lax.dynamic_index_in_dim(regrid_target, position, 0, keepdims=False)
    surface = jnp.dot(
        ocean_state.reshape(tokens, channels), surface_read, preferred_element_type=jnp.float32
    ).astype(jnp.bfloat16)
    surfaces = lax.all_gather(surface[None, :], "lon", axis=0, tiled=True)
    picked = jnp.take(surfaces, targets, axis=0)
    lifted = jnp.einsum("kcd,kd->c", blocks, picked, preferred_element_type=jnp.float32)
    state = (
        atmosphere.astype(jnp.float32) + lifted.reshape(height, width)[..., None] * surface_embed
    ).astype(jnp.bfloat16)
    full_projection, full_output = (
        lax.all_gather(projection, "lon", axis=0, tiled=True),
        lax.all_gather(output_weight, "lon", axis=0, tiled=True),
    )
    edges = from_behind((state[:, :shift], cotangent[:, :shift]), "lon", -1)
    shifted = jnp.concatenate([state[:, shift:], edges[0]], axis=1)
    grad_shifted = jnp.concatenate([cotangent[:, shift:], edges[1]], axis=1)
    normed = layer_norm(shifted.astype(jnp.float32), attention_gain).astype(jnp.bfloat16)
    normed_flat = normed.reshape(tokens, model)
    packed = (
        jnp.dot(normed_flat, full_projection, preferred_element_type=jnp.float32)
        .astype(jnp.bfloat16)
        .reshape(height, width, 3 * model)
    )
    packed_windows = to_windows(packed, WIN)
    mixed, probs, weights = attend_forward(packed_windows, heads, HEAD_DIM)
    attended = from_windows(mixed, height, width, WIN)
    attended_flat = attended.reshape(tokens, model)
    change = jnp.dot(attended_flat, full_output, preferred_element_type=jnp.float32).reshape(
        height, width, model
    )
    updated = (shifted.astype(jnp.float32) + change).astype(jnp.bfloat16)
    moved = from_behind(updated[:, width - shift :], "lon", 1)
    atmosphere_out = jnp.concatenate([moved, updated[:, : width - shift]], axis=1)
    flux = jnp.dot(
        atmosphere_out.reshape(tokens, model), flux_weight, preferred_element_type=jnp.float32
    ).astype(jnp.bfloat16)
    pieces = jnp.einsum("cf,kcd->kfd", flux, blocks, preferred_element_type=jnp.float32)
    routing = (targets[:, None] == jnp.arange(devices, dtype=jnp.int32)[None, :]).astype(
        jnp.float32
    )
    outgoing = jnp.einsum("kt,kfd->tfd", routing, pieces, precision=HIGHEST)
    arrived = lax.psum_scatter(outgoing, "lon", scatter_dimension=0, tiled=True)[0]
    forcing = jnp.dot(arrived.T, flux_embed, precision=HIGHEST).reshape(height, width, channels)
    forced = (ocean_state.astype(jnp.float32) + forcing).astype(jnp.bfloat16)
    reach = KERNEL // 2
    margin = extended(forced, (("lon", 1),), reach)
    padded = jnp.pad(margin.astype(jnp.float32), ((reach, reach), (0, 0), (0, 0)))
    conv = depthwise_conv(padded, depthwise, height, width)
    ocean_normed = layer_norm(conv, ocean_gain).astype(jnp.bfloat16)
    hidden = jax.nn.gelu(
        jnp.dot(ocean_normed.reshape(tokens, channels), expand, preferred_element_type=jnp.float32)
    ).astype(jnp.bfloat16)
    ocean_change = jnp.dot(hidden, contract, preferred_element_type=jnp.float32).reshape(
        height, width, channels
    )
    ocean_next = (
        ocean_state.astype(jnp.float32) + ocean_mask.astype(jnp.float32)[..., None] * ocean_change
    ).astype(jnp.bfloat16)
    grad_flat = grad_shifted.reshape(tokens, model)
    grad_att = (
        lax.dot_general(
            grad_flat, full_output, (((1,), (1,)), ((), ())), preferred_element_type=jnp.float32
        )
        .astype(jnp.bfloat16)
        .reshape(height, width, model)
    )
    grad_packed = attend_backward(
        packed_windows, probs, weights, to_windows(grad_att, WIN), heads, HEAD_DIM
    )
    grad_grid = from_windows(grad_packed, height, width, WIN).reshape(tokens, 3 * model)
    weight_grad = lax.psum_scatter(
        jnp.concatenate(
            [
                transposed_product(normed_flat, grad_grid),
                transposed_product(attended_flat, grad_flat),
            ],
            axis=1,
        ),
        "lon",
        scatter_dimension=0,
        tiled=True,
    )
    return (atmosphere_out, ocean_next, weight_grad)


def solution(mesh):
    return jax.shard_map(
        per_device,
        mesh=mesh,
        in_specs=(
            P("groups", "lon", None),
            P("groups", "lon", None),
            P("groups", "lon", None),
            P("groups", "lon"),
            P("lon", None),
            P("lon", None),
            P(),
            P(),
            P(),
            P(),
            P(),
            P(),
            P(),
            P(),
            P(),
            P("lon", None, None, None),
            P(),
        ),
        out_specs=(P("groups", "lon", None), P("groups", "lon", None), P(("groups", "lon"), None)),
        check_vma=False,
    )
```

profile of v0, /device:TPU:0, one launch (start us, length us, event | category | flops | bytes accessed | tf_op | source)
XLA Modules:
  0.0 492.9 jit_solution(232981658921982704)
XLA Ops:
  7.2 0.7 all-gather.7.cloned.1.call-update
  8.0 0.7 all-gather.5.cloned.1.call-update
  8.7 0.7 reshape.283
  9.4 1.1 fusion.184
  10.6 23.1 %all-gather.1 = bf16[16,1,256]{2,1,0:T(2,128)(2,1)S(1)} all-gather(bf16[1,1,256]{2,1,0:T(2,128)(2,1)S(1)} %reshape.280), channel_id=2, replica_groups=mesh['groups'=2,'lon'=16] {'lon'}, dimensions={0}, use_global_device_ids=true | all-gather | bytes 8704 | tf_op jit(solution)/shard_map/all_gather | solution.py:154
  33.7 0.9 dynamic-slice_reduce_fusion
  34.6 0.6 gather_fusion
  35.2 1.2 fusion.149
  36.4 1.2 add_convert_fusion
  37.8 0.9 slice.445
  38.9 0.9 slice.444
  39.8 0.9 collective-permute-done
  40.9 0.3 multiply_reduce_fusion.2
  41.4 1.1 collective-permute-done.4
  42.6 1.1 pad_maximum_fusion.3
  43.7 1.0 fusion.51
  44.8 1.1 multiply_convert_fusion.1
  45.9 8.7 %all-gather.7.cloned.1.call-done = bf16[1024,1024]{1,0:T(8,128)(2,1)} async-done(((bf16[64,1024]{1,0:T(8,128)(2,1)}), bf16[1024,1024]{1,0:T(8,128)(2,1)}) %all-gather.7.cloned.1.call-update) | async-done | bytes 2097168 | tf_op jit(solution)/shard_map/all_gather | solution.py:162
  54.5 2.3 convolution_convert_fusion.3
  56.9 0.8 copy.137
  57.7 3.8 reshape_reshape.17
  61.5 4.0 copy.101
  65.5 53.0 %all-gather.5.cloned.1.call-done = bf16[1024,3072]{1,0:T(8,128)(2,1)} async-done(((bf16[64,3072]{1,0:T(8,128)(2,1)}), bf16[1024,3072]{1,0:T(8,128)(2,1)}) %all-gather.5.cloned.1.call-update) | async-done | bytes 6291472 | tf_op jit(solution)/shard_map/all_gather | solution.py:161
  118.6 4.6 convolution_convert_fusion
  123.3 1.1 fusion.176
  124.4 2.4 copy.93
  126.8 2.4 copy.92
  129.2 1.3 copy.91
  130.5 4.3 fusion.185
  134.7 5.2 %fusion.181 = (f32[4,32,64]{2,1,0:T(8,128)S(1)}, f32[4,32,64,64]{2,3,1,0:T(8,128)}) fusion(bf16[4,64,32,32]{1,3,2,0:T(8,128)(2,1)} %bitcast.192, bf16[4,64,32,32]{1,3,2,0:T(8,128)(2,1)} %bitcast.190), kind=kOutput, calls=%fused_computation.249 | convolution fusion | flops 35127360 | bytes 3178496 | tf_op jit(solution)/shard_map/sub | solution.py:66
  140.0 8.4 %fusion.38 = bf16[4,64,32,32]{1,3,2,0:T(8,128)(2,1)} fusion(bf16[4,64,32,32]{1,3,2,0:T(8,128)(2,1)} %bitcast.191, f32[4,32,64,64]{2,3,1,0:T(8,128)} %fusion.185, f32[4,32,64,64]{2,3,1,0:T(8,128)} %get-tuple-element.60, f32[4,32,64]{2,1,0:T(8,128)S(1)} %get-tuple-element.59), kind=kOutput, calls=%fused_computation.79 | convolution fusion | flops 37494848 | bytes 5275648 | tf_op jit(solution)/shard_map/whqk,wkhd->wqhd/dot_general | solution.py:88
  148.4 8.6 %fusion.35 = bf16[4,64,32,32]{1,3,2,0:T(8,128)(2,1)} fusion(bf16[4,64,32,32]{1,3,2,0:T(8,128)(2,1)} %bitcast.193, f32[4,32,64,64]{2,3,1,0:T(8,128)} %fusion.185, f32[4,32,64,64]{2,3,1,0:T(8,128)} %get-tuple-element.60, f32[4,32,64]{2,1,0:T(8,128)S(1)} %get-tuple-element.59), kind=kOutput, calls=%fused_computation.78 | convolution fusion | flops 37494848 | bytes 5275648 | tf_op jit(solution)/shard_map/whqk,wqhd->wkhd/dot_general | solution.py:91
  157.1 4.8 fusion.34
  161.9 1.6 fusion.33
  163.5 4.7 copy.95
  168.2 4.2 convert_element_type.119
  172.5 1.1 copy.96
  173.6 2.5 fusion.44
  176.1 0.8 copy-done.8
  176.9 0.3 collective-permute-start.1
  177.2 4.7 copy.108
  181.9 3.5 concatenate.38
  185.4 4.7 copy.105
  190.2 4.2 concatenate.37
  194.4 4.7 copy.103
  199.1 4.2 concatenate.36
  203.3 1.4 maximum_bitcast_fusion
  204.8 6.4 %fusion.186 = f32[1024,3072]{1,0:T(8,128)} fusion(bf16[256,1024]{1,0:T(8,128)(2,1)S(1)} %bitcast.182, bf16[256,3072]{1,0:T(8,128)(2,1)S(1)} %bitcast.178), kind=kOutput, calls=%fused_computation.253 | convolution fusion | flops 1610612736 | bytes 14680064 | tf_op jit(solution)/shard_map/dot_general | solution.py:118
  211.2 2.7 fusion.187
  214.1 0.5 convolution_bitcast_fusion
  214.9 0.7 copy.98
  215.6 11.9 %pad_maximum_fusion = f32[1024,4096]{1,0:T(8,128)} fusion(f32[1024,1024]{1,0:T(8,128)} %fusion.187, f32[1024,3072]{1,0:T(8,128)} %fusion.186), kind=kLoop, calls=%fused_computation.3 | loop fusion | flops 4194304 | bytes 33554432 | tf_op jit(solution)/shard_map/concatenate | solution.py:222
  227.6 0.6 copy-done.18
  228.2 0.6 dynamic-slice
  228.9 72.2 %all-reduce.4.cloned.1.call-done = f32[16,4,256]{2,1,0:T(4,128)} async-done(((f32[16,4,256]{2,1,0:T(4,128)}), f32[16,4,256]{2,1,0:T(4,128)}) %all-reduce.4.cloned.1.call-update) | async-done | bytes 65552
  301.1 1.3 dynamic-slice_bitcast_fusion
  302.5 0.6 fusion.47
  303.2 0.4 collective-permute-start.2
  303.6 4.1 collective-permute-start.3
  307.7 1.5 collective-permute-done.2
  309.4 3.7 fusion.174
  313.5 3.2 fusion.54
  316.7 0.8 fusion.56
  317.5 168.8 %reduce-scatter.2.cloned.1.call-done = f32[64,4096]{1,0:T(8,128)} async-done(((f32[1024,4096]{1,0:T(8,128)}), f32[64,4096]{1,0:T(8,128)}) %reduce-scatter.2.cloned.1.call-update) | async-done | bytes 1048592 | tf_op jit(solution)/shard_map/reduce_scatter | solution.py:221
  (78 shorter events, 2.4 us)
Async XLA Ops:
  7.2 306.3 %copy-start = (bf16[2048,512]{1,0:T(8,128)(2,1)S(1)}, bf16[2048,512]{1,0:T(8,128)(2,1)}, u32[]{:S(2)}) copy-start(bf16[2048,512]{1,0:T(8,128)(2,1)} %param.31) | copy-start | bytes 6291460
  7.2 31.7 %copy-start.7 = (bf16[8,32,1024]{2,1,0:T(8,128)(2,1)S(1)}, bf16[8,32,1024]{2,1,0:T(8,128)(2,1)}, u32[]{:S(2)}) copy-start(bf16[8,32,1024]{2,1,0:T(8,128)(2,1)} %param.18) | copy-start | bytes 1572868
  7.2 47.3 %all-gather.7.cloned.1.call-start = ((), (), s32[]{:S(2)}) async-start(), calls=%async_computation.2 | async-start | bytes 2228224 | tf_op jit(solution)/shard_map/all_gather | solution.py:162
  7.9 110.6 %all-gather.5.cloned.1.call-start = ((), (), s32[]{:S(2)}) async-start(), calls=%async_computation.1 | async-start | bytes 6684672 | tf_op jit(solution)/shard_map/all_gather | solution.py:161
  8.7 292.4 %all-reduce.4.cloned.1.call-start = ((), (), s32[]{:S(2)}) async-start(), calls=%async_computation.4 | async-start | bytes 131072
  9.4 34.3 %copy-start.13 = (f32[1024]{0:T(1024)S(1)}, f32[1024]{0:T(1024)}, u32[]{:S(2)}) copy-start(f32[1024]{0:T(1024)} %param.23) | copy-start | bytes 12292
  37.7 3.0 collective-permute-start
  38.7 3.9 collective-permute-start.4
  43.7 14.0 %copy-start.4 = (bf16[8,32,1024]{2,1,0:T(8,128)(2,1)}, bf16[8,32,1024]{2,1,0:T(8,128)(2,1)S(1)}, u32[]{:S(2)}) copy-start(bf16[8,32,1024]{2,1,0:T(8,128)(2,1)S(1)} %pad_maximum_fusion.3) | copy-start | bytes 1572868
  57.7 60.9 %copy-start.10 = (bf16[256,1024]{1,0:T(8,128)(2,1)S(1)}, bf16[256,1024]{1,0:T(8,128)(2,1)}, u32[]{:S(2)}) copy-start(bf16[256,1024]{1,0:T(8,128)(2,1)} %fusion.51) | copy-start | bytes 1572868
  157.0 4.8 copy-start.1
  157.0 4.8 copy-start.19
  176.1 0.8 copy-start.8
  176.9 37.0 %collective-permute-start.1 = (bf16[8,4,1024]{2,1,0:T(4,128)(2,1)S(1)}, bf16[8,4,1024]{2,1,0:T(4,128)(2,1)S(1)}, u32[]{:S(2)}, u32[]{:S(2)}) collective-permute-start(bf16[8,4,1024]{2,1,0:T(4,128)(2,1)S(1)} %slice.453), channel_id=1, source_target_pairs={{15,0},{0,1},{1,2},{2,3},{3,4},{4,5},{5,6},{6,7},{7,8},{8,9},{9,10... | collective-permute-start | bytes 196616 | tf_op jit(solution)/shard_map/ppermute | solution.py:18
  203.3 1.5 copy-start.2
  204.8 6.4 %copy-start.5 = (bf16[8,32,1024]{2,1,0:T(8,128)(2,1)S(1)}, bf16[8,32,1024]{2,1,0:T(8,128)(2,1)}, u32[]{:S(2)}) copy-start(bf16[8,32,1024]{2,1,0:T(8,128)(2,1)} %copy-done.4) | copy-start | bytes 1572868
  211.2 2.7 copy-start.9
  211.2 2.9 copy-start.11
  211.2 2.9 copy-start.14
  214.1 13.5 %copy-start.6 = (bf16[8,32,1024]{2,1,0:T(8,128)(2,1)}, bf16[8,32,1024]{2,1,0:T(8,128)(2,1)S(1)}, u32[]{:S(2)}) copy-start(bf16[8,32,1024]{2,1,0:T(8,128)(2,1)S(1)} %pad_maximum_fusion.2) | copy-start | bytes 1572868
  215.6 270.8 %reduce-scatter.2.cloned.1.call-start = ((), (), s32[]{:S(2)}) async-start(), calls=%async_computation.3 | async-start | bytes 17825792 | tf_op jit(solution)/shard_map/reduce_scatter | solution.py:221
  227.6 0.7 copy-start.18
  227.6 1.3 copy-start.12
  227.6 74.9 %copy-start.3 = (bf16[8,32,512]{2,1,0:T(8,128)(2,1)S(1)}, bf16[8,32,512]{2,1,0:T(8,128)(2,1)}, u32[]{:S(2)}) copy-start(bf16[8,32,512]{2,1,0:T(8,128)(2,1)} %param.19) | copy-start | bytes 786436
  227.6 74.9 %copy-start.15 = (f32[4,512]{1,0:T(4,128)S(1)}, f32[4,512]{1,0:T(4,128)}, u32[]{:S(2)}) copy-start(f32[4,512]{1,0:T(4,128)} %param.27) | copy-start | bytes 24580
  227.6 80.1 %copy-start.16 = (s32[8,32]{1,0:T(8,128)S(1)}, s32[8,32]{1,0:T(8,128)}, u32[]{:S(2)}) copy-start(s32[8,32]{1,0:T(8,128)} %param.20) | copy-start | bytes 3076
  303.2 6.1 %collective-permute-start.2 = (bf16[8,3,512]{2,1,0:T(4,128)(2,1)S(1)}, bf16[8,3,512]{2,1,0:T(4,128)(2,1)S(1)}, u32[]{:S(2)}, u32[]{:S(2)}) collective-permute-start(bf16[8,3,512]{2,1,0:T(4,128)(2,1)S(1)} %get-tuple-element.8), channel_id=1, source_target_pairs={{0,1},{1,2},{2,3},{3,4},{4,5},{5,6},{6,7},{7,8},{8,9},{9,10},{10,1... | collective-permute-start | bytes 73736 | tf_op jit(solution)/shard_map/ppermute | solution.py:28
  303.6 5.7 %collective-permute-start.3 = (bf16[8,3,512]{2,1,0:T(4,128)(2,1)S(1)}, bf16[8,3,512]{2,1,0:T(4,128)(2,1)S(1)}, u32[]{:S(2)}, u32[]{:S(2)}) collective-permute-start(bf16[8,3,512]{2,1,0:T(4,128)(2,1)S(1)} %get-tuple-element.9), channel_id=1, source_target_pairs={{1,0},{2,1},{3,2},{4,3},{5,4},{6,5},{7,6},{8,7},{9,8},{10,9},{11,1... | collective-permute-start | bytes 73736 | tf_op jit(solution)/shard_map/ppermute | solution.py:29
  307.7 5.6 %copy-start.17 = (f32[512]{0:T(512)S(1)}, f32[512]{0:T(512)}, u32[]{:S(2)}) copy-start(f32[512]{0:T(512)} %param.29) | copy-start | bytes 6148
Sparse Core Ops, SparseCore 0:
  10.2 44.2 all-gather.6
  56.8 61.7 all-gather.4
  215.7 85.3 all-reduce.3
  306.2 180.1 reduce-scatter.1
where the time goes:
time: 494 us; the launch traced here: 493 us
  waiting for transfers between devices  308 us (62%)
  local copies, waits for them, and re-layouts  60.8 us (12%)
  matrix products  58.4 us (12%)
  other arithmetic  23.6 us (5%)
  blocking collectives  23.1 us (5%)
  between operations  14.2 us (3%)
  starting transfers between devices  5.08 us (1%)
    reduce_scatter x1, waiting for transfers between devices, per_device(): lax.psum_scatter(jnp.concatenate([transposed_product(normed_flat, grad_gr...  169 us
    unnamed x5, waiting for transfers between devices  73.6 us
    all_gather x1, waiting for transfers between devices, per_device(): lax.all_gather(projection, 'lon', axis=0, tiled=True)  53 us
    all_gather x1, blocking collectives, per_device(): surfaces = lax.all_gather(surface[None, :], 'lon', axis=0, tiled=True)  23.1 us
    concatenate x3, local copies, waits for them, and re-layouts, attend_backward(): jnp.concatenate([grad_query.reshape(windows, tokens, width), grad_keys.re...  12 us
    concatenate x1, other arithmetic, per_device(): jnp.concatenate([transposed_product(normed_flat, grad_grid), transposed_p...  11.9 us
  transfers between devices with their start and end apart: 9, of which 7 were waited for; matrix products, arithmetic and copies ran while one was open for 17% of the time, Pallas kernels for 0%

commit v1 on v0

v1 whole, which is shorter than its diff:
```python
import functools

import jax
import jax.numpy as jnp
from jax import lax
from jax.experimental import pallas as pl
from jax.experimental.pallas import tpu as pltpu
from jax.sharding import PartitionSpec as P

HEAD_DIM = 32
WIN = 8
KERNEL = 7
LANES = 4
PACK = 4


EPSILON = 1e-05
HIGHEST = lax.Precision.HIGHEST
MESH = pl.DeviceIdType.MESH


def from_behind(block, axis, distance):
    devices = range(lax.axis_size(axis))
    route = [((i - distance) % len(devices), i) for i in devices]
    return lax.ppermute(block, axis, route)


def extended(shard, sides, width):
    for axis, dim in sides:
        peers, length = (lax.axis_size(axis), shard.shape[dim])
        up = [(i, (i + 1) % peers) for i in range(peers)]
        down = [(j, i) for i, j in up]
        last = lax.slice_in_dim(shard, length - width, length, axis=dim)
        leading = lax.slice_in_dim(shard, 0, width, axis=dim)
        before = lax.ppermute(last, axis, up)
        after = lax.ppermute(leading, axis, down)
        shard = jnp.concatenate([before, shard, after], axis=dim)
    return shard


def layer_norm(values, gain):
    center = values - jnp.mean(values, axis=-1, keepdims=True)
    spread = jnp.mean(center * center, axis=-1, keepdims=True)
    return center * lax.rsqrt(spread + EPSILON) * gain


def to_windows(values, window):
    height, width, depth = values.shape
    blocks = values.reshape(height // window, window, width // window, window, depth)
    return blocks.transpose(0, 2, 1, 3, 4).reshape(-1, depth)


def from_windows(values, height, width, window):
    depth = values.shape[-1]
    blocks = values.reshape(height // window, width // window, window, window, depth)
    return blocks.transpose(0, 2, 1, 3, 4).reshape(height, width, depth)


def ring_place(chip, chips):
    if chips != 8:
        return chip
    return (chip % 2) * (chips - 1 - chip // 2) + (1 - chip % 2) * (chip // 2)


def ring_chip(place, chips):
    if chips != 8:
        return place
    back = place // (chips // 2)
    return (1 - back) * (2 * place) + back * (2 * (chips - 1 - place) + 1)


def meet_all(n, me):
    barrier = pltpu.get_barrier_semaphore()

    def greet(offset, carry):
        pl.semaphore_signal(
            barrier, inc=1, device_id={"lon": (me + offset) % n}, device_id_type=MESH
        )
        return carry

    lax.fori_loop(1, n, greet, 0)
    pl.semaphore_wait(barrier, n - 1)


def direct_copy(src, dst, sems, offset, peer):
    return pltpu.make_async_remote_copy(
        src_ref=src,
        dst_ref=dst,
        send_sem=sems.at[0, offset],
        recv_sem=sems.at[1, offset],
        device_id={"lon": peer},
        device_id_type=MESH,
    )


def small_gather_kernel(n, x_ref, out_ref, sems):
    me = lax.axis_index("lon")
    meet_all(n, me)

    def send(offset, carry):
        direct_copy(x_ref, out_ref.at[me], sems, offset, (me + offset) % n).start()
        return carry

    def wait(offset, carry):
        copy = direct_copy(x_ref, out_ref.at[(me + n - offset) % n], sems, offset, (me + offset) % n)
        copy.wait()
        return carry

    lax.fori_loop(1, n, send, 0)
    out_ref[me] = x_ref[...]
    lax.fori_loop(1, n, wait, 0)


def small_gather(x, n, collective_id):
    return pl.pallas_call(
        functools.partial(small_gather_kernel, n),
        out_shape=jax.ShapeDtypeStruct((n,) + x.shape, x.dtype),
        in_specs=[pl.BlockSpec(memory_space=pltpu.VMEM)],
        out_specs=pl.BlockSpec(memory_space=pltpu.VMEM),
        scratch_shapes=[pltpu.SemaphoreType.DMA((2, n))],
        compiler_params=pltpu.CompilerParams(collective_id=collective_id, has_side_effects=True),
    )(x)


def gather_weights_kernel(
    n, proj_ref, out_weight_ref, surface_ref, w_ref, s_ref, ring_sems, pair_sems, own_sems, near_sems
):
    rows, width = out_weight_ref.shape
    chips = n // 2
    me = lax.axis_index("lon")
    core = me % 2
    place = ring_place(me // 2, chips)
    sibling = me + 1 - 2 * core

    own = []
    for lane in range(LANES):
        src = proj_ref.at[:, pl.ds(lane * width, width)] if lane < LANES - 1 else out_weight_ref
        own.append(
            pltpu.make_async_copy(
                src, w_ref.at[pl.ds(me * rows, rows), pl.ds(lane * width, width)], own_sems.at[lane]
            )
        )
        own[-1].start()
    own.append(pltpu.make_async_copy(surface_ref, s_ref.at[me], own_sems.at[LANES]))
    own[-1].start()
    meet_all(n, me)

    def send_near(offset, carry):
        direct_copy(surface_ref, s_ref.at[me], near_sems, offset, (me + offset) % n).start()
        return carry

    def wait_near(offset, carry):
        direct_copy(
            surface_ref, s_ref.at[(me + n - offset) % n], near_sems, offset, (me + offset) % n
        ).wait()
        return carry

    def slot(lane, distance, half):
        owner = ring_chip((place + distance) % chips, chips) * 2 + half
        return w_ref.at[
            pl.ds(pl.multiple_of(owner * rows, rows), rows), pl.ds(lane * width, width)
        ]

    def behind(lane, step):
        return step if lane % 2 else chips - step

    def ring_copy(lane, step, distance):
        ahead = chips - 1 if lane % 2 else 1
        block = slot(lane, distance, core)
        return pltpu.make_async_remote_copy(
            src_ref=block,
            dst_ref=block,
            send_sem=ring_sems.at[0, lane, step],
            recv_sem=ring_sems.at[1, lane, step],
            device_id={"lon": ring_chip((place + ahead) % chips, chips) * 2 + core},
            device_id_type=MESH,
        )

    def pair_copy(lane, step, half):
        block = slot(lane, behind(lane, step), half)
        return pltpu.make_async_remote_copy(
            src_ref=block,
            dst_ref=block,
            send_sem=pair_sems.at[0, lane, step],
            recv_sem=pair_sems.at[1, lane, step],
            device_id={"lon": sibling},
            device_id_type=MESH,
        )

    for copy in own:
        copy.wait()
    for lane in range(LANES):
        ring_copy(lane, 0, behind(lane, 0)).start()
    lax.fori_loop(1, n, send_near, 0)
    for lane in range(LANES):
        pair_copy(lane, 0, core).start()

    def step_on(step, carry):
        for lane in range(LANES):
            ring_copy(lane, step - 1, behind(lane, step)).wait_recv()
            ring_copy(lane, step, behind(lane, step)).start()
            pair_copy(lane, step, core).start()
        return carry

    lax.fori_loop(1, chips - 1, step_on, 0)
    for lane in range(LANES):
        ring_copy(lane, chips - 2, behind(lane, chips - 1)).wait_recv()
        pair_copy(lane, chips - 1, core).start()

    def drain(step, carry):
        for lane in range(LANES):
            ring_copy(lane, step, behind(lane, step)).wait_send()
        return carry

    def drain_pair(step, carry):
        for lane in range(LANES):
            pair_copy(lane, step, core).wait_send()
            pair_copy(lane, step, 1 - core).wait_recv()
        return carry

    lax.fori_loop(1, n, wait_near, 0)
    lax.fori_loop(0, chips - 1, drain, 0)
    lax.fori_loop(0, chips, drain_pair, 0)


def gather_weights(projection, output_weight, surface, n):
    rows, width = output_weight.shape
    chips = n // 2
    anywhere = pl.BlockSpec(memory_space=pl.ANY)
    return pl.pallas_call(
        functools.partial(gather_weights_kernel, n),
        out_shape=(
            jax.ShapeDtypeStruct((n * rows, LANES * width), projection.dtype),
            jax.ShapeDtypeStruct((n,) + surface.shape, surface.dtype),
        ),
        in_specs=[anywhere] * 3,
        out_specs=(anywhere, anywhere),
        scratch_shapes=[
            pltpu.SemaphoreType.DMA((2, LANES, chips - 1)),
            pltpu.SemaphoreType.DMA((2, LANES, chips)),
            pltpu.SemaphoreType.DMA((LANES + 1,)),
            pltpu.SemaphoreType.DMA((2, n)),
        ],
        compiler_params=pltpu.CompilerParams(collective_id=0, has_side_effects=True),
    )(projection, output_weight, surface)


def attention_kernel(packed_ref, grad_ref, attended_ref, grad_packed_ref):
    tokens, model = grad_ref.shape
    lanes = PACK * HEAD_DIM
    spread = PACK * tokens
    row_head = lax.broadcasted_iota(jnp.int32, (spread, lanes), 0) // tokens
    column_head = lax.broadcasted_iota(jnp.int32, (spread, lanes), 1) // HEAD_DIM
    own_head = row_head == column_head
    head_of = lax.broadcasted_iota(jnp.int32, (tokens, lanes), 1) // HEAD_DIM
    lower = lax.broadcasted_iota(jnp.int32, (tokens, 2 * tokens), 1) < tokens

    def expand_heads(block):
        tiled = jnp.concatenate([block] * PACK, axis=0)
        return jnp.where(own_head, tiled, jnp.zeros_like(tiled))

    def collapse_heads(block):
        total = jnp.where(head_of == 0, block[:tokens], 0.0)
        for head in range(1, PACK):
            total = total + jnp.where(head_of == head, block[head * tokens : (head + 1) * tokens], 0.0)
        return total

    def per_head(values, reduce, neutral):
        parts = []
        for start in range(0, spread, 2 * tokens):
            part = values[:, start : start + 2 * tokens]
            low = reduce(jnp.where(lower, part, neutral), axis=1, keepdims=True)
            high = reduce(jnp.where(lower, neutral, part), axis=1, keepdims=True)
            parts.append(jnp.where(lower, low, high))
        return jnp.concatenate(parts, axis=1)

    def product(left, right, contract):
        return lax.dot_general(
            left, right, (contract, ((), ())), preferred_element_type=jnp.float32
        )

    last, first = ((1,), (1,)), ((0,), (0,))
    plain = ((1,), (0,))
    scale = HEAD_DIM ** (-0.5)
    for group in range(model // lanes):
        at = group * lanes
        query = packed_ref[:, at : at + lanes]
        keys = expand_heads(packed_ref[:, model + at : model + at + lanes])
        values = expand_heads(packed_ref[:, 2 * model + at : 2 * model + at + lanes])
        grad = grad_ref[:, at : at + lanes]
        scores = product(query, keys, last) * scale
        powers = jnp.exp(scores - per_head(scores, jnp.max, -jnp.inf))
        probs = powers / per_head(powers, jnp.sum, 0.0)
        weights = probs.astype(jnp.bfloat16)
        attended_ref[:, at : at + lanes] = product(weights, values, plain).astype(jnp.bfloat16)
        grad_probs = product(grad, values, last)
        grad_values = collapse_heads(product(weights, grad, first))
        inner = per_head(grad_probs * probs, jnp.sum, 0.0)
        grad_scores = (probs * (grad_probs - inner) * scale).astype(jnp.bfloat16)
        grad_query = product(grad_scores, keys, plain)
        grad_keys = collapse_heads(product(grad_scores, query, first))
        grad_packed_ref[:, at : at + lanes] = grad_query.astype(jnp.bfloat16)
        grad_packed_ref[:, model + at : model + at + lanes] = grad_keys.astype(jnp.bfloat16)
        grad_packed_ref[:, 2 * model + at : 2 * model + at + lanes] = grad_values.astype(jnp.bfloat16)


def attention(packed, grad_att):
    tokens, model = grad_att.shape
    cells = WIN * WIN
    wide = pl.BlockSpec((cells, 3 * model), lambda w: (w, 0))
    narrow = pl.BlockSpec((cells, model), lambda w: (w, 0))
    return pl.pallas_call(
        attention_kernel,
        grid=(tokens // cells,),
        out_shape=(
            jax.ShapeDtypeStruct((tokens, model), jnp.bfloat16),
            jax.ShapeDtypeStruct((tokens, 3 * model), jnp.bfloat16),
        ),
        in_specs=[wide, narrow],
        out_specs=(narrow, wide),
        compiler_params=pltpu.CompilerParams(vmem_limit_bytes=48 * 1024 * 1024),
        cost_estimate=pl.CostEstimate(
            flops=14 * tokens * cells * model * PACK,
            bytes_accessed=16 * tokens * model,
            transcendentals=tokens * cells * (model // HEAD_DIM),
        ),
    )(packed, grad_att)


def depthwise_conv(padded, kernel, height, width):
    reach = kernel.shape[0]
    total = jnp.zeros((height, width, kernel.shape[2]), jnp.float32)
    for row in range(reach):
        for column in range(reach):
            total = (
                total + padded[row : row + height, column : column + width] * kernel[row, column]
            )
    return total


def dot32(left, right):
    return jnp.dot(left, right, preferred_element_type=jnp.float32)


def largest(values):
    return jnp.max(jnp.abs(values)).astype(jnp.float32)


def reduce_ring(terms, scale, forward, devices, position):
    chips = devices // 2
    core = position % 2
    place = ring_place(position // 2, chips)
    step_by = 1 if forward else -1
    route = []
    for device in range(devices):
        ahead = ring_chip((ring_place(device // 2, chips) + step_by) % chips, chips)
        route.append((device, ahead * 2 + device % 2))

    def term(distance):
        chip = ring_chip((place + step_by * distance + 2 * chips) % chips, chips)
        return lax.dynamic_index_in_dim(terms, chip, 0, keepdims=False) * scale

    moving = term(-1).astype(jnp.float16)
    for step in range(chips - 1):
        moving = lax.ppermute(moving, "lon", route).astype(jnp.float32) + term(-2 - step)
        if step < chips - 2:
            moving = moving.astype(jnp.float16)
    return moving / scale


def per_device(
    atmosphere,
    cotangent,
    ocean_state,
    ocean_mask,
    projection,
    output_weight,
    attention_gain,
    surface_embed,
    surface_read,
    flux_weight,
    flux_embed,
    depthwise,
    ocean_gain,
    expand,
    contract,
    regrid_blocks,
    regrid_target,
):
    height, width, model = atmosphere.shape
    channels = ocean_state.shape[2]
    shift = WIN // 2
    tokens = height * width
    devices = lax.axis_size("lon")
    position = lax.axis_index("lon")
    chips = devices // 2
    core = position % 2
    blocks = regrid_blocks[0]
    targets = lax.dynamic_index_in_dim(regrid_target, position, 0, keepdims=False)
    surface = dot32(ocean_state.reshape(tokens, channels), surface_read).astype(jnp.bfloat16)
    all_weights, surfaces = gather_weights(
        projection,
        output_weight,
        jnp.broadcast_to(surface.astype(jnp.float32)[None], (8, tokens)),
        devices,
    )
    picked = jnp.take(surfaces[:, 0], targets, axis=0).astype(jnp.bfloat16)
    lifted = jnp.einsum("kcd,kd->c", blocks, picked, preferred_element_type=jnp.float32)
    state = (
        atmosphere.astype(jnp.float32) + lifted.reshape(height, width)[..., None] * surface_embed
    ).astype(jnp.bfloat16)
    full_projection, full_output = all_weights[:, : 3 * model], all_weights[:, 3 * model :]
    edges = (
        from_behind(state[:, :shift], "lon", -1),
        from_behind(cotangent[:, :shift], "lon", -1),
    )
    shifted = to_windows(jnp.concatenate([state[:, shift:], edges[0]], axis=1), WIN)
    grad_flat = to_windows(jnp.concatenate([cotangent[:, shift:], edges[1]], axis=1), WIN)
    normed = layer_norm(shifted.astype(jnp.float32), attention_gain).astype(jnp.bfloat16)
    packed = dot32(normed, full_projection).astype(jnp.bfloat16)
    grad_att = lax.dot_general(
        grad_flat, full_output, (((1,), (1,)), ((), ())), preferred_element_type=jnp.float32
    ).astype(jnp.bfloat16)
    attended, grad_packed = attention(packed, grad_att)

    bound = tokens * jnp.maximum(
        largest(normed) * largest(grad_packed), largest(attended) * largest(grad_flat)
    )
    bounds = small_gather(jnp.full((8, 128), bound, jnp.float32), devices, 1)
    scale = 30000.0 / jnp.maximum(jnp.sum(bounds[:, 0, 0]), 1e-30)

    pairs = [(i, i + 1 - 2 * (i % 2)) for i in range(devices)]

    def split_rows(values):
        turned = values.T.reshape(chips, 2, model // devices, tokens)
        mine = lax.dynamic_index_in_dim(turned, core, 1, keepdims=False)
        other = lax.dynamic_index_in_dim(turned, 1 - core, 1, keepdims=False)
        mine, other = (part.reshape(model // 2, tokens) for part in (mine, other))
        return mine, lax.ppermute(other, "lon", pairs)

    normed_rows = split_rows(normed)
    attended_rows = split_rows(attended)
    rights = [grad_packed[:, i * model : (i + 1) * model] for i in range(3)] + [grad_flat]
    reduced = []
    for lane, right in enumerate(rights):
        rows = normed_rows if lane < 3 else attended_rows
        far = lax.ppermute(right, "lon", pairs)
        terms = (dot32(rows[0], right) + dot32(rows[1], far)).reshape(chips, -1, model)
        reduced.append(reduce_ring(terms, scale, lane % 2 == 0, devices, position))
    weight_grad = jnp.concatenate(reduced, axis=1)

    change = dot32(attended, full_output)
    updated = from_windows(
        (shifted.astype(jnp.float32) + change).astype(jnp.bfloat16), height, width, WIN
    )
    moved = from_behind(updated[:, width - shift :], "lon", 1)
    atmosphere_out = jnp.concatenate([moved, updated[:, : width - shift]], axis=1)
    flux = dot32(atmosphere_out.reshape(tokens, model), flux_weight).astype(jnp.bfloat16)
    pieces = jnp.einsum("cf,kcd->kfd", flux, blocks, preferred_element_type=jnp.float32)
    fluxes = flux_weight.shape[1]
    every = small_gather(pieces.reshape(2 * fluxes, tokens), devices, 2)
    every = every.reshape(devices, 2, fluxes, tokens)
    here = (regrid_target == position)[:, :, None, None]
    arrived = jnp.sum(jnp.where(here, every, 0.0), axis=(0, 1))
    forcing = jnp.dot(arrived.T, flux_embed, precision=HIGHEST).reshape(height, width, channels)
    forced = (ocean_state.astype(jnp.float32) + forcing).astype(jnp.bfloat16)
    reach = KERNEL // 2
    margin = extended(forced, (("lon", 1),), reach)
    padded = jnp.pad(margin.astype(jnp.float32), ((reach, reach), (0, 0), (0, 0)))
    conv = depthwise_conv(padded, depthwise, height, width)
    ocean_normed = layer_norm(conv, ocean_gain).astype(jnp.bfloat16)
    hidden = jax.nn.gelu(dot32(ocean_normed.reshape(tokens, channels), expand)).astype(jnp.bfloat16)
    ocean_change = dot32(hidden, contract).reshape(height, width, channels)
    ocean_next = (
        ocean_state.astype(jnp.float32) + ocean_mask.astype(jnp.float32)[..., None] * ocean_change
    ).astype(jnp.bfloat16)
    return (atmosphere_out, ocean_next, weight_grad)


def solution(mesh):
    return jax.shard_map(
        per_device,
        mesh=mesh,
        in_specs=(
            P("groups", "lon", None),
            P("groups", "lon", None),
            P("groups", "lon", None),
            P("groups", "lon"),
            P("lon", None),
            P("lon", None),
            P(),
            P(),
            P(),
            P(),
            P(),
            P(),
            P(),
            P(),
            P(),
            P("lon", None, None, None),
            P(),
        ),
        out_specs=(P("groups", "lon", None), P("groups", "lon", None), P(("groups", "lon"), None)),
        check_vma=False,
    )
```

time: 494 us -> 230 us (0.47)
  waiting for transfers between devices: 308 us -> 14.6 us
  Pallas kernels: 0 us -> 99.7 us
  local copies, waits for them, and re-layouts: 60.8 us -> 19.1 us
  starting transfers between devices: 5.08 us -> 39.4 us
  matrix products: 58.4 us -> 31.5 us
  blocking collectives: 23.1 us -> 0 us
  between operations: 14.2 us -> 5.21 us
    reduce_scatter x1 -> x0, waiting for transfers between devices: 169 us -> none  [per_device(): lax.psum_scatter(jnp.concatenate([transposed_product(normed_flat, grad_gr...]
    pallas_call x0 -> x4, Pallas kernels: none -> 99.7 us  [the longest x1 66.4 us: gather_weights(): pl.pallas_call(functools.partial(gather_weights_kernel, n), out_shape=(ja...]
    unnamed x5 -> x0, waiting for transfers between devices: 73.6 us -> none
    all_gather x2 -> x0, waiting for transfers between devices: 61.7 us -> none  [the longest x1 53 us: per_device(): lax.all_gather(projection, 'lon', axis=0, tiled=True)]
    ppermute x0 -> x34, starting transfers between devices: none -> 32.3 us  [the longest x28 30.9 us: reduce_ring(): lax.ppermute(moving, 'lon', route).astype(jnp.float32) + term(-2 - step)]
    all_gather x1 -> x0, blocking collectives: 23.1 us -> none  [per_device(): surfaces = lax.all_gather(surface[None, :], 'lon', axis=0, tiled=True)]
    dot_general x12, matrix products: 48.5 us -> 25.4 us  [dot32(): return jnp.dot(left, right, preferred_element_type=jnp.float32)]
    concatenate x2 -> x1, other arithmetic: 13.1 us -> 1.04 us  [per_device(): weight_grad = jnp.concatenate(reduced, axis=1)]
  transfers between devices with their start and end apart: 9 -> 39, of which waited for: 7 -> 22; matrix products, arithmetic and copies ran while one was open for 17% -> 26% of each run, Pallas kernels for 0% -> 15%
where the time goes in v1:
time: 230 us; the launch traced here: 229 us
  Pallas kernels  99.7 us (43%)
  starting transfers between devices  39.4 us (17%)
  matrix products  31.5 us (14%)
  other arithmetic  19.2 us (8%)
  local copies, waits for them, and re-layouts  19.1 us (8%)
  waiting for transfers between devices  14.6 us (6%)
  between operations  5.21 us (2%)
    pallas_call x1, Pallas kernels, gather_weights(): pl.pallas_call(functools.partial(gather_weights_kernel, n), out_shape=(ja...  66.4 us
    ppermute x28, starting transfers between devices, reduce_ring(): lax.ppermute(moving, 'lon', route).astype(jnp.float32) + term(-2 - step)  30.9 us
    dot_general x12, matrix products, dot32(): return jnp.dot(left, right, preferred_element_type=jnp.float32)  25.4 us
    pallas_call x2, Pallas kernels, small_gather(): pl.pallas_call(functools.partial(small_gather_kernel, n), out_shape=jax.S...  17.9 us
    pallas_call x1, Pallas kernels, attention(): pl.pallas_call(attention_kernel, grid=(tokens // cells,), out_shape=(jax....  15.4 us
    ppermute x28, waiting for transfers between devices, reduce_ring(): lax.ppermute(moving, 'lon', route).astype(jnp.float32) + term(-2 - step)  11.2 us
    reduce_sum x2, other arithmetic, layer_norm(): center = values - jnp.mean(values, axis=-1, keepdims=True)  5.01 us
  transfers between devices with their start and end apart: 39, of which 22 were waited for; matrix products, arithmetic and copies ran while one was open for 26% of the time, Pallas kernels for 15%

profile of v1, /device:TPU:0, one launch (start us, length us, event | category | flops | bytes accessed | tf_op | source)
XLA Modules:
  0.0 228.8 jit_solution(3021529404359812671)
XLA Ops:
  0.7 1.0 fusion.165
  1.7 0.7 reshape.284
  2.4 1.1 fusion.187
  4.2 66.4 %shard_map.184 = (bf16[1024,4096]{1,0:T(8,128)(2,1)}, f32[16,8,256]{2,1,0:T(8,128)}) custom-call(bf16[64,3072]{1,0:T(8,128)(2,1)} %proj_ref.1, bf16[64,1024]{1,0:T(8,128)(2,1)} %out_weight_ref.1, f32[8,256]{1,0:T(8,128)} %broadcast_in_dim.45.surface_ref), custom_call_target="tpu_custom_call" | custom-call | tf_op jit(solution)/shard_map/pallas_call | solution.py:230
  70.6 0.9 slice.346
  72.2 1.3 fusion.156
  73.5 1.2 add_convert_fusion
  74.8 2.5 %collective-permute-start = (bf16[8,4,1024]{2,1,0:T(4,128)(2,1)S(1)}, bf16[8,4,1024]{2,1,0:T(4,128)(2,1)S(1)}, u32[]{:S(2)}, u32[]{:S(2)}) collective-permute-start(bf16[8,4,1024]{2,1,0:T(4,128)(2,1)S(1)} %slice.462), channel_id=1, source_target_pairs={{1,0},{2,1},{3,2},{4,3},{5,4},{6,5},{7,6},{8,7},{9,8},{10,9},{11,1... | collective-permute-start | bytes 196616 | tf_op jit(solution)/shard_map/ppermute | solution.py:25
  77.2 0.9 slice.351
  79.0 0.7 fusion.182
  79.7 0.7 fusion.183
  82.1 1.1 fusion.126
  83.3 2.4 %copy.36 = f32[1,8,4,8,1024]{4,3,1,2,0:T(8,128)} copy(f32[1,8,4,8,1024]{4,3,2,1,0:T(8,128)} %fusion.126) | data formatting | bytes 2097152 | tf_op jit(solution)/shard_map/convert_element_type | solution.py:454
  85.8 0.7 abs_reduce_fusion.1
  86.5 0.8 copy.37
  87.7 2.6 %fusion.20.grad_ref = bf16[256,1024]{1,0:T(8,128)(2,1)S(1)} fusion(bf16[256,1024]{1,0:T(8,128)(2,1)} %bitcast.15, bf16[1024,4096]{1,0:T(8,128)(2,1)} %get-tuple-element.8), kind=kOutput, calls=%fused_computation.65 | convolution fusion | flops 537133056 | bytes 3145728 | tf_op jit(solution)/shard_map/dot_general | solution.py:421
  90.3 1.0 fusion.30
  91.3 4.8 %fusion.2.packed_ref = bf16[256,3072]{1,0:T(8,128)(2,1)S(1)} fusion(bf16[256,1024]{1,0:T(8,128)(2,1)} %fusion.30, bf16[1024,4096]{1,0:T(8,128)(2,1)} %get-tuple-element.8), kind=kOutput, calls=%fused_computation.45 | convolution fusion | flops 1611399168 | bytes 8388608 | tf_op jit(solution)/shard_map/dot_general | solution.py:342
  96.1 15.4 %shard_map.185 = (bf16[256,1024]{1,0:T(8,128)(2,1)S(1)}, bf16[256,3072]{1,0:T(8,128)(2,1)S(1)}) custom-call(bf16[256,3072]{1,0:T(8,128)(2,1)S(1)} %fusion.2.packed_ref, bf16[256,1024]{1,0:T(8,128)(2,1)S(1)} %fusion.20.grad_ref), custom_call_target="tpu_custom_call" | custom-call | flops 939524096 | bytes 4194304 | tf_op jit(solution)/shard_map/pallas_call | solution.py:312
  111.5 0.9 abs_reduce_fusion
  112.5 1.2 fusion.180
  113.7 0.7 abs_reduce_fusion.2
  114.4 1.0 copy.42
  115.4 2.1 copy.41
  117.4 2.2 constant_dynamic-slice_fusion
  119.7 1.7 fusion.172
  121.4 1.8 fusion.174
  123.2 1.8 fusion.176
  125.0 2.3 %fusion.23 = bf16[256,1024]{1,0:T(8,128)(2,1)S(1)} fusion(f32[256,1024]{1,0:T(8,128)S(1)} %bitcast.315, bf16[256,1024]{1,0:T(8,128)(2,1)S(1)} %get-tuple-element.9, bf16[1024,4096]{1,0:T(8,128)(2,1)} %get-tuple-element.8), kind=kOutput, calls=%fused_computation.66 | convolution fusion | flops 537395200 | bytes 4194304 | tf_op jit(solution)/shard_map/dot_general | solution.py:342
  127.4 0.7 slice.463
  128.2 2.8 %fusion.188 = f32[512,1024]{1,0:T(8,128)} fusion(bf16[512,256]{1,0:T(8,128)(2,1)S(1)} %bitcast.325, bf16[256,1024]{1,0:T(8,128)(2,1)} %bitcast.15), kind=kOutput, calls=%fused_computation.304 | convolution fusion | flops 268435456 | bytes 2883584 | tf_op jit(solution)/shard_map/dot_general | solution.py:342
  131.1 0.9 fusion.35
  134.9 8.8 %shard_map.187 = f32[16,8,128]{2,1,0:T(8,128)} custom-call(f32[8,128]{1,0:T(8,128)} %broadcast_in_dim.51.x_ref), custom_call_target="tpu_custom_call" | custom-call | tf_op jit(solution)/shard_map/pallas_call | solution.py:115
  143.8 1.0 pad_maximum_fusion.1
  144.8 1.6 convolution_bitcast_fusion
  147.0 9.0 %shard_map.186 = f32[16,8,256]{2,1,0:T(8,128)} custom-call(f32[8,256]{1,0:T(8,128)} %reshape.260.x_ref), custom_call_target="tpu_custom_call" | custom-call | tf_op jit(solution)/shard_map/pallas_call | solution.py:115
  156.0 1.0 select_reduce_fusion
  157.9 4.3 %collective-permute-start.4 = (bf16[8,3,512]{2,1,0:T(4,128)(2,1)S(1)}, bf16[8,3,512]{2,1,0:T(4,128)(2,1)S(1)}, u32[]{:S(2)}, u32[]{:S(2)}) collective-permute-start(bf16[8,3,512]{2,1,0:T(4,128)(2,1)S(1)} %get-tuple-element.23), channel_id=1, source_target_pairs={{1,0},{2,1},{3,2},{4,3},{5,4},{6,5},{7,6},{8,7},{9,8},{10,9},{11,1... | collective-permute-start | bytes 73736 | tf_op jit(solution)/shard_map/ppermute | solution.py:36
  162.2 1.5 slice_reduce_fusion
  164.9 3.3 %collective-permute-done.3 = bf16[8,3,512]{2,1,0:T(4,128)(2,1)S(1)} collective-permute-done((bf16[8,3,512]{2,1,0:T(4,128)(2,1)S(1)}, bf16[8,3,512]{2,1,0:T(4,128)(2,1)S(1)}, u32[]{:S(2)}, u32[]{:S(2)}) %collective-permute-start.3) | collective-permute-done | bytes 24608 | tf_op jit(solution)/shard_map/ppermute | solution.py:35
  168.3 4.8 %fusion.178 = (f32[8,32]{1,0:T(8,128)S(1)}, f32[8,32,512]{2,1,0:T(8,128)S(1)}) fusion(f32[512]{0:T(512)} %bitcast.342, f32[512]{0:T(512)} %bitcast.343, f32[512]{0:T(512)} %bitcast.345, f32[512]{0:T(512)} %bitcast.346, f32[512]{0:T(512)} %bitcast.347, f32[512]{0:T(512)} %bitcast.348, f32[512]{0:T(512)} %bitcast.349, f32[512]{0:T(512)} %bitcast.350, ...), kind=kLoop, calls=%fused_computation.296 | loop fusion | flops 12844800 | bytes 4951040 | tf_op jit(solution)/shard_map/reduce_sum | solution.py:42
  173.6 3.2 %fusion.31 = f32[256,512]{1,0:T(8,128)S(1)} fusion(bf16[2048,512]{1,0:T(8,128)(2,1)S(1)} %copy-done, bf16[256,512]{1,0:T(8,128)(2,1)S(1)} %bitcast.329, bf16[512,2048]{1,0:T(8,128)(2,1)} %param.30), kind=kOutput, calls=%fused_computation.82 | convolution fusion | flops 1078460416 | bytes 4980736 | tf_op jit(solution)/shard_map/dot_general | solution.py:342
  176.7 0.8 fusion.33
  178.1 2.4 %convolution_add_fusion = f32[512,1024]{1,0:T(8,128)S(1)} fusion(f32[512,1024]{1,0:T(8,128)} %fusion.188, bf16[512,256]{1,0:T(8,128)(2,1)} %collective-permute-done.30, bf16[256,1024]{1,0:T(8,128)(2,1)} %collective-permute-done.31), kind=kOutput, calls=%fused_computation.59 | convolution fusion | flops 268959744 | bytes 4980736 | tf_op jit(solution)/shard_map/dot_general | solution.py:342
  180.6 1.6 convolution_add_fusion.1
  182.3 1.9 collective-permute-start.23
  184.2 1.5 convolution_add_fusion.2
  186.4 1.9 collective-permute-start.7
  188.7 1.9 collective-permute-start.24
  190.6 1.0 collective-permute-done.15
  191.9 0.8 collective-permute-done.7
  192.7 2.1 collective-permute-start.8
  195.5 2.0 collective-permute-start.25
  198.8 1.6 collective-permute-start.9
  201.9 2.0 collective-permute-start.26
  204.7 2.1 collective-permute-start.10
  208.2 2.0 collective-permute-start.27
  211.2 2.0 collective-permute-start.11
  214.3 1.8 collective-permute-start.28
  217.3 2.0 collective-permute-start.12
  220.4 2.1 collective-permute-start.29
  222.7 2.0 collective-permute-start.13
  224.8 2.8 %collective-permute-done.21 = f16[64,1024]{1,0:T(8,128)(2,1)S(1)} collective-permute-done((f16[64,1024]{1,0:T(8,128)(2,1)S(1)}, f16[64,1024]{1,0:T(8,128)(2,1)S(1)}, u32[]{:S(2)}, u32[]{:S(2)}) %collective-permute-start.21) | collective-permute-done | bytes 131104 | tf_op jit(solution)/shard_map/ppermute | solution.py:365
  227.7 1.0 pad_maximum_fusion
  (162 shorter events, 19.3 us)
Async XLA Ops:
  0.6 172.9 %copy-start = (bf16[2048,512]{1,0:T(8,128)(2,1)S(1)}, bf16[2048,512]{1,0:T(8,128)(2,1)}, u32[]{:S(2)}) copy-start(bf16[2048,512]{1,0:T(8,128)(2,1)} %param.31) | copy-start | bytes 6291460
  0.6 79.7 %copy-start.16 = (s32[16,2]{0,1:T(2,128)S(1)}, s32[16,2]{0,1:T(2,128)}, u32[]{:S(2)}) copy-start(s32[16,2]{0,1:T(2,128)} %param.33) | copy-start | bytes 388
  0.7 77.7 %copy-start.11 = (f32[7,7,512]{2,1,0:T(8,128)S(1)}, f32[7,7,512]{2,1,0:T(8,128)}, u32[]{:S(2)}) copy-start(f32[7,7,512]{2,1,0:T(8,128)} %param.28) | copy-start | bytes 301060
  72.1 8.4 %copy-start.10 = (bf16[8,32,1024]{2,1,0:T(8,128)(2,1)S(1)}, bf16[8,32,1024]{2,1,0:T(8,128)(2,1)}, u32[]{:S(2)}) copy-start(bf16[8,32,1024]{2,1,0:T(8,128)(2,1)} %param.18) | copy-start | bytes 1572868
  74.7 6.8 %copy-start.15 = (s32[8,32]{1,0:T(8,128)S(1)}, s32[8,32]{1,0:T(8,128)}, u32[]{:S(2)}) copy-start(s32[8,32]{1,0:T(8,128)} %param.20) | copy-start | bytes 3076
  74.8 6.8 %collective-permute-start = (bf16[8,4,1024]{2,1,0:T(4,128)(2,1)S(1)}, bf16[8,4,1024]{2,1,0:T(4,128)(2,1)S(1)}, u32[]{:S(2)}, u32[]{:S(2)}) collective-permute-start(bf16[8,4,1024]{2,1,0:T(4,128)(2,1)S(1)} %slice.462), channel_id=1, source_target_pairs={{1,0},{2,1},{3,2},{4,3},{5,4},{6,5},{7,6},{8,7},{9,8},{10,9},{11,1... | collective-permute-start | bytes 196616 | tf_op jit(solution)/shard_map/ppermute | solution.py:25
  78.2 7.6 %collective-permute-start.1 = (bf16[8,4,1024]{2,1,0:T(4,128)(2,1)S(1)}, bf16[8,4,1024]{2,1,0:T(4,128)(2,1)S(1)}, u32[]{:S(2)}, u32[]{:S(2)}) collective-permute-start(bf16[8,4,1024]{2,1,0:T(4,128)(2,1)S(1)} %slice.351), channel_id=1, source_target_pairs={{1,0},{2,1},{3,2},{4,3},{5,4},{6,5},{7,6},{8,7},{9,8},{10,9},{11,1... | collective-permute-start | bytes 196616 | tf_op jit(solution)/shard_map/ppermute | solution.py:25
  87.3 90.7 %collective-permute-start.31 = (bf16[256,1024]{1,0:T(8,128)(2,1)}, bf16[256,1024]{1,0:T(8,128)(2,1)}, u32[]{:S(2)}, u32[]{:S(2)}) collective-permute-start(bf16[256,1024]{1,0:T(8,128)(2,1)} %bitcast.15), channel_id=1, source_target_pairs={{0,1},{1,0},{2,3},{3,2},{4,5},{5,4},{6,7},{7,6},{8,9},{9,8},{10,11... | collective-permute-start | bytes 1572872 | tf_op jit(solution)/shard_map/ppermute | solution.py:447
  87.7 2.6 %copy-start.6 = (f32[1,8,4,8,1024]{4,3,1,2,0:T(8,128)S(1)}, f32[1,8,4,8,1024]{4,3,1,2,0:T(8,128)}, u32[]{:S(2)}) copy-start(f32[1,8,4,8,1024]{4,3,1,2,0:T(8,128)} %copy.36) | copy-start | bytes 3145732
  87.7 2.6 %copy-start.12 = (f32[1024]{0:T(1024)S(1)}, f32[1024]{0:T(1024)}, u32[]{:S(2)}) copy-start(f32[1024]{0:T(1024)} %param.23) | copy-start | bytes 12292
  111.5 2.2 copy-start.1
  117.4 2.2 copy-start.2
  123.2 1.8 copy-start.7
  128.1 15.7 %collective-permute-start.2 = (bf16[8,4,1024]{2,1,0:T(4,128)(2,1)}, bf16[8,4,1024]{2,1,0:T(4,128)(2,1)}, u32[]{:S(2)}, u32[]{:S(2)}) collective-permute-start(bf16[8,4,1024]{2,1,0:T(4,128)(2,1)} %slice.463), channel_id=1, source_target_pairs={{15,0},{0,1},{1,2},{2,3},{3,4},{4,5},{5,6},{6,7},{7,8},{8,9},{9,10... | collective-permute-start | bytes 196616 | tf_op jit(solution)/shard_map/ppermute | solution.py:25
  128.2 16.6 %copy-start.13 = (bf16[1024,4]{0,1:T(4,128)(2,1)S(1)}, bf16[1024,4]{0,1:T(4,128)(2,1)}, u32[]{:S(2)}) copy-start(bf16[1024,4]{0,1:T(4,128)(2,1)} %param.26) | copy-start | bytes 24580
  131.1 26.1 %copy-start.8 = (bf16[8,32,512]{2,1,0:T(8,128)(2,1)S(1)}, bf16[8,32,512]{2,1,0:T(8,128)(2,1)}, u32[]{:S(2)}) copy-start(bf16[8,32,512]{2,1,0:T(8,128)(2,1)} %param.19) | copy-start | bytes 786436
  131.1 26.1 %copy-start.14 = (f32[4,512]{1,0:T(4,128)S(1)}, f32[4,512]{1,0:T(4,128)}, u32[]{:S(2)}) copy-start(f32[4,512]{1,0:T(4,128)} %param.27) | copy-start | bytes 24580
  131.1 46.5 %collective-permute-start.30 = (bf16[512,256]{1,0:T(8,128)(2,1)}, bf16[512,256]{1,0:T(8,128)(2,1)}, u32[]{:S(2)}, u32[]{:S(2)}) collective-permute-start(bf16[512,256]{1,0:T(8,128)(2,1)} %bitcast.111), channel_id=1, source_target_pairs={{0,1},{1,0},{2,3},{3,2},{4,5},{5,4},{6,7},{7,6},{8,9},{9,8},{10,11... | collective-permute-start | bytes 786440 | tf_op jit(solution)/shard_map/ppermute | solution.py:439
  144.8 23.5 %copy-start.9 = (bf16[8,32,1024]{2,1,0:T(8,128)(2,1)}, bf16[8,32,1024]{2,1,0:T(8,128)(2,1)S(1)}, u32[]{:S(2)}) copy-start(bf16[8,32,1024]{2,1,0:T(8,128)(2,1)S(1)} %pad_maximum_fusion.1) | copy-start | bytes 1572868
  157.9 6.5 %collective-permute-start.4 = (bf16[8,3,512]{2,1,0:T(4,128)(2,1)S(1)}, bf16[8,3,512]{2,1,0:T(4,128)(2,1)S(1)}, u32[]{:S(2)}, u32[]{:S(2)}) collective-permute-start(bf16[8,3,512]{2,1,0:T(4,128)(2,1)S(1)} %get-tuple-element.23), channel_id=1, source_target_pairs={{1,0},{2,1},{3,2},{4,3},{5,4},{6,5},{7,6},{8,7},{9,8},{10,9},{11,1... | collective-permute-start | bytes 73736 | tf_op jit(solution)/shard_map/ppermute | solution.py:36
  162.1 6.0 %collective-permute-start.3 = (bf16[8,3,512]{2,1,0:T(4,128)(2,1)S(1)}, bf16[8,3,512]{2,1,0:T(4,128)(2,1)S(1)}, u32[]{:S(2)}, u32[]{:S(2)}) collective-permute-start(bf16[8,3,512]{2,1,0:T(4,128)(2,1)S(1)} %get-tuple-element.22), channel_id=1, source_target_pairs={{0,1},{1,2},{2,3},{3,4},{4,5},{5,6},{6,7},{7,8},{8,9},{9,10},{10,1... | collective-permute-start | bytes 73736 | tf_op jit(solution)/shard_map/ppermute | solution.py:35
  163.6 17.0 %collective-permute-start.5 = (bf16[512,256]{1,0:T(8,128)(2,1)}, bf16[512,256]{1,0:T(8,128)(2,1)S(1)}, u32[]{:S(2)}, u32[]{:S(2)}) collective-permute-start(bf16[512,256]{1,0:T(8,128)(2,1)} %bitcast.330), channel_id=1, source_target_pairs={{0,1},{1,0},{2,3},{3,2},{4,5},{5,4},{6,7},{7,6},{8,9},{9,8},{10,11... | collective-permute-start | bytes 786440 | tf_op jit(solution)/shard_map/ppermute | solution.py:439
  164.3 16.3 %collective-permute-start.22 = (bf16[256,1024]{1,0:T(8,128)(2,1)}, bf16[256,1024]{1,0:T(8,128)(2,1)}, u32[]{:S(2)}, u32[]{:S(2)}) collective-permute-start(bf16[256,1024]{1,0:T(8,128)(2,1)} %get-tuple-element.16), channel_id=1, source_target_pairs={{0,1},{1,0},{2,3},{3,2},{4,5},{5,4},{6,7},{7,6},{8,9},{9,8},{10,11... | collective-permute-start | bytes 1572872 | tf_op jit(solution)/shard_map/ppermute | solution.py:447
  168.2 16.0 %collective-permute-start.14 = (bf16[256,1024]{1,0:T(8,128)(2,1)}, bf16[256,1024]{1,0:T(8,128)(2,1)}, u32[]{:S(2)}, u32[]{:S(2)}) collective-permute-start(bf16[256,1024]{1,0:T(8,128)(2,1)} %get-tuple-element.17), channel_id=1, source_target_pairs={{0,1},{1,0},{2,3},{3,2},{4,5},{5,4},{6,7},{7,6},{8,9},{9,8},{10,11... | collective-permute-start | bytes 1572872 | tf_op jit(solution)/shard_map/ppermute | solution.py:447
  168.3 5.1 %copy-start.17 = (f32[512]{0:T(512)S(1)}, f32[512]{0:T(512)}, u32[]{:S(2)}) copy-start(f32[512]{0:T(512)} %param.29) | copy-start | bytes 6148
  177.6 3.0 %copy-start.5 = (f32[512,1024]{1,0:T(8,128)S(1)}, f32[512,1024]{1,0:T(8,128)}, u32[]{:S(2)}) copy-start(f32[512,1024]{1,0:T(8,128)} %fusion.172) | copy-start | bytes 6291460
  177.6 8.4 %collective-permute-start.6 = (bf16[256,1024]{1,0:T(8,128)(2,1)}, bf16[256,1024]{1,0:T(8,128)(2,1)S(1)}, u32[]{:S(2)}, u32[]{:S(2)}) collective-permute-start(bf16[256,1024]{1,0:T(8,128)(2,1)} %get-tuple-element.15), channel_id=1, source_target_pairs={{0,1},{1,0},{2,3},{3,2},{4,5},{5,4},{6,7},{7,6},{8,9},{9,8},{10,11... | collective-permute-start | bytes 1572872 | tf_op jit(solution)/shard_map/ppermute | solution.py:447
  180.5 3.7 %copy-start.4 = (f32[512,1024]{1,0:T(8,128)S(1)}, f32[512,1024]{1,0:T(8,128)}, u32[]{:S(2)}) copy-start(f32[512,1024]{1,0:T(8,128)} %fusion.174) | copy-start | bytes 6291460
  180.5 7.8 %collective-permute-start.32 = (f16[64,1024]{1,0:T(8,128)(2,1)S(1)}, f16[64,1024]{1,0:T(8,128)(2,1)S(1)}, u32[]{:S(2)}, u32[]{:S(2)}) collective-permute-start(f16[64,1024]{1,0:T(8,128)(2,1)S(1)} %fusion.161), channel_id=1, source_target_pairs={{0,2},{1,3},{2,6},{3,7},{4,0},{5,1},{6,10},{7,11},{8,4},{9,5},{10,... | collective-permute-start | bytes 393224 | tf_op jit(solution)/shard_map/ppermute | solution.py:365
  182.3 3.7 %copy-start.3 = (f32[512,1024]{1,0:T(8,128)S(1)}, f32[512,1024]{1,0:T(8,128)}, u32[]{:S(2)}) copy-start(f32[512,1024]{1,0:T(8,128)} %fusion.176) | copy-start | bytes 6291460
  182.3 6.3 %collective-permute-start.23 = (f16[64,1024]{1,0:T(8,128)(2,1)S(1)}, f16[64,1024]{1,0:T(8,128)(2,1)S(1)}, u32[]{:S(2)}, u32[]{:S(2)}) collective-permute-start(f16[64,1024]{1,0:T(8,128)(2,1)S(1)} %fusion.160), channel_id=1, source_target_pairs={{0,4},{1,5},{2,0},{3,1},{4,8},{5,9},{6,2},{7,3},{8,12},{9,13},{10,... | collective-permute-start | bytes 393224 | tf_op jit(solution)/shard_map/ppermute | solution.py:365
  185.7 5.9 %collective-permute-start.15 = (f16[64,1024]{1,0:T(8,128)(2,1)S(1)}, f16[64,1024]{1,0:T(8,128)(2,1)S(1)}, u32[]{:S(2)}, u32[]{:S(2)}) collective-permute-start(f16[64,1024]{1,0:T(8,128)(2,1)S(1)} %fusion.159), channel_id=1, source_target_pairs={{0,2},{1,3},{2,6},{3,7},{4,0},{5,1},{6,10},{7,11},{8,4},{9,5},{10,... | collective-permute-start | bytes 393224 | tf_op jit(solution)/shard_map/ppermute | solution.py:365
  186.4 6.2 %collective-permute-start.7 = (f16[64,1024]{1,0:T(8,128)(2,1)S(1)}, f16[64,1024]{1,0:T(8,128)(2,1)S(1)}, u32[]{:S(2)}, u32[]{:S(2)}) collective-permute-start(f16[64,1024]{1,0:T(8,128)(2,1)S(1)} %fusion.158), channel_id=1, source_target_pairs={{0,4},{1,5},{2,0},{3,1},{4,8},{5,9},{6,2},{7,3},{8,12},{9,13},{10,... | collective-permute-start | bytes 393224 | tf_op jit(solution)/shard_map/ppermute | solution.py:365
  188.4 6.5 %collective-permute-start.33 = (f16[64,1024]{1,0:T(8,128)(2,1)S(1)}, f16[64,1024]{1,0:T(8,128)(2,1)S(1)}, u32[]{:S(2)}, u32[]{:S(2)}) collective-permute-start(f16[64,1024]{1,0:T(8,128)(2,1)S(1)} %fusion.133), channel_id=1, source_target_pairs={{0,2},{1,3},{2,6},{3,7},{4,0},{5,1},{6,10},{7,11},{8,4},{9,5},{10,... | collective-permute-start | bytes 393224 | tf_op jit(solution)/shard_map/ppermute | solution.py:365
  188.7 6.8 %collective-permute-start.24 = (f16[64,1024]{1,0:T(8,128)(2,1)S(1)}, f16[64,1024]{1,0:T(8,128)(2,1)S(1)}, u32[]{:S(2)}, u32[]{:S(2)}) collective-permute-start(f16[64,1024]{1,0:T(8,128)(2,1)S(1)} %fusion.140), channel_id=1, source_target_pairs={{0,4},{1,5},{2,0},{3,1},{4,8},{5,9},{6,2},{7,3},{8,12},{9,13},{10,... | collective-permute-start | bytes 393224 | tf_op jit(solution)/shard_map/ppermute | solution.py:365
  191.6 6.2 %collective-permute-start.16 = (f16[64,1024]{1,0:T(8,128)(2,1)S(1)}, f16[64,1024]{1,0:T(8,128)(2,1)S(1)}, u32[]{:S(2)}, u32[]{:S(2)}) collective-permute-start(f16[64,1024]{1,0:T(8,128)(2,1)S(1)} %fusion.147), channel_id=1, source_target_pairs={{0,2},{1,3},{2,6},{3,7},{4,0},{5,1},{6,10},{7,11},{8,4},{9,5},{10,... | collective-permute-start | bytes 393224 | tf_op jit(solution)/shard_map/ppermute | solution.py:365
  192.7 6.0 %collective-permute-start.8 = (f16[64,1024]{1,0:T(8,128)(2,1)S(1)}, f16[64,1024]{1,0:T(8,128)(2,1)S(1)}, u32[]{:S(2)}, u32[]{:S(2)}) collective-permute-start(f16[64,1024]{1,0:T(8,128)(2,1)S(1)} %fusion.154), channel_id=1, source_target_pairs={{0,4},{1,5},{2,0},{3,1},{4,8},{5,9},{6,2},{7,3},{8,12},{9,13},{10,... | collective-permute-start | bytes 393224 | tf_op jit(solution)/shard_map/ppermute | solution.py:365
  194.9 5.8 %collective-permute-start.34 = (f16[64,1024]{1,0:T(8,128)(2,1)S(1)}, f16[64,1024]{1,0:T(8,128)(2,1)S(1)}, u32[]{:S(2)}, u32[]{:S(2)}) collective-permute-start(f16[64,1024]{1,0:T(8,128)(2,1)S(1)} %fusion.132), channel_id=1, source_target_pairs={{0,2},{1,3},{2,6},{3,7},{4,0},{5,1},{6,10},{7,11},{8,4},{9,5},{10,... | collective-permute-start | bytes 393224 | tf_op jit(solution)/shard_map/ppermute | solution.py:365
  195.5 6.3 %collective-permute-start.25 = (f16[64,1024]{1,0:T(8,128)(2,1)S(1)}, f16[64,1024]{1,0:T(8,128)(2,1)S(1)}, u32[]{:S(2)}, u32[]{:S(2)}) collective-permute-start(f16[64,1024]{1,0:T(8,128)(2,1)S(1)} %fusion.139), channel_id=1, source_target_pairs={{0,4},{1,5},{2,0},{3,1},{4,8},{5,9},{6,2},{7,3},{8,12},{9,13},{10,... | collective-permute-start | bytes 393224 | tf_op jit(solution)/shard_map/ppermute | solution.py:365
  197.9 6.2 %collective-permute-start.17 = (f16[64,1024]{1,0:T(8,128)(2,1)S(1)}, f16[64,1024]{1,0:T(8,128)(2,1)S(1)}, u32[]{:S(2)}, u32[]{:S(2)}) collective-permute-start(f16[64,1024]{1,0:T(8,128)(2,1)S(1)} %fusion.146), channel_id=1, source_target_pairs={{0,2},{1,3},{2,6},{3,7},{4,0},{5,1},{6,10},{7,11},{8,4},{9,5},{10,... | collective-permute-start | bytes 393224 | tf_op jit(solution)/shard_map/ppermute | solution.py:365
  198.8 5.8 %collective-permute-start.9 = (f16[64,1024]{1,0:T(8,128)(2,1)S(1)}, f16[64,1024]{1,0:T(8,128)(2,1)S(1)}, u32[]{:S(2)}, u32[]{:S(2)}) collective-permute-start(f16[64,1024]{1,0:T(8,128)(2,1)S(1)} %fusion.153), channel_id=1, source_target_pairs={{0,4},{1,5},{2,0},{3,1},{4,8},{5,9},{6,2},{7,3},{8,12},{9,13},{10,... | collective-permute-start | bytes 393224 | tf_op jit(solution)/shard_map/ppermute | solution.py:365
  200.8 6.3 %collective-permute-start.35 = (f16[64,1024]{1,0:T(8,128)(2,1)S(1)}, f16[64,1024]{1,0:T(8,128)(2,1)S(1)}, u32[]{:S(2)}, u32[]{:S(2)}) collective-permute-start(f16[64,1024]{1,0:T(8,128)(2,1)S(1)} %fusion.131), channel_id=1, source_target_pairs={{0,2},{1,3},{2,6},{3,7},{4,0},{5,1},{6,10},{7,11},{8,4},{9,5},{10,... | collective-permute-start | bytes 393224 | tf_op jit(solution)/shard_map/ppermute | solution.py:365
  201.9 6.3 %collective-permute-start.26 = (f16[64,1024]{1,0:T(8,128)(2,1)S(1)}, f16[64,1024]{1,0:T(8,128)(2,1)S(1)}, u32[]{:S(2)}, u32[]{:S(2)}) collective-permute-start(f16[64,1024]{1,0:T(8,128)(2,1)S(1)} %fusion.138), channel_id=1, source_target_pairs={{0,4},{1,5},{2,0},{3,1},{4,8},{5,9},{6,2},{7,3},{8,12},{9,13},{10,... | collective-permute-start | bytes 393224 | tf_op jit(solution)/shard_map/ppermute | solution.py:365
  204.2 6.2 %collective-permute-start.18 = (f16[64,1024]{1,0:T(8,128)(2,1)S(1)}, f16[64,1024]{1,0:T(8,128)(2,1)S(1)}, u32[]{:S(2)}, u32[]{:S(2)}) collective-permute-start(f16[64,1024]{1,0:T(8,128)(2,1)S(1)} %fusion.145), channel_id=1, source_target_pairs={{0,2},{1,3},{2,6},{3,7},{4,0},{5,1},{6,10},{7,11},{8,4},{9,5},{10,... | collective-permute-start | bytes 393224 | tf_op jit(solution)/shard_map/ppermute | solution.py:365
  204.7 6.5 %collective-permute-start.10 = (f16[64,1024]{1,0:T(8,128)(2,1)S(1)}, f16[64,1024]{1,0:T(8,128)(2,1)S(1)}, u32[]{:S(2)}, u32[]{:S(2)}) collective-permute-start(f16[64,1024]{1,0:T(8,128)(2,1)S(1)} %fusion.152), channel_id=1, source_target_pairs={{0,4},{1,5},{2,0},{3,1},{4,8},{5,9},{6,2},{7,3},{8,12},{9,13},{10,... | collective-permute-start | bytes 393224 | tf_op jit(solution)/shard_map/ppermute | solution.py:365
  207.2 6.2 %collective-permute-start.36 = (f16[64,1024]{1,0:T(8,128)(2,1)S(1)}, f16[64,1024]{1,0:T(8,128)(2,1)S(1)}, u32[]{:S(2)}, u32[]{:S(2)}) collective-permute-start(f16[64,1024]{1,0:T(8,128)(2,1)S(1)} %fusion.130), channel_id=1, source_target_pairs={{0,2},{1,3},{2,6},{3,7},{4,0},{5,1},{6,10},{7,11},{8,4},{9,5},{10,... | collective-permute-start | bytes 393224 | tf_op jit(solution)/shard_map/ppermute | solution.py:365
  208.2 6.0 %collective-permute-start.27 = (f16[64,1024]{1,0:T(8,128)(2,1)S(1)}, f16[64,1024]{1,0:T(8,128)(2,1)S(1)}, u32[]{:S(2)}, u32[]{:S(2)}) collective-permute-start(f16[64,1024]{1,0:T(8,128)(2,1)S(1)} %fusion.137), channel_id=1, source_target_pairs={{0,4},{1,5},{2,0},{3,1},{4,8},{5,9},{6,2},{7,3},{8,12},{9,13},{10,... | collective-permute-start | bytes 393224 | tf_op jit(solution)/shard_map/ppermute | solution.py:365
  210.4 6.0 %collective-permute-start.19 = (f16[64,1024]{1,0:T(8,128)(2,1)S(1)}, f16[64,1024]{1,0:T(8,128)(2,1)S(1)}, u32[]{:S(2)}, u32[]{:S(2)}) collective-permute-start(f16[64,1024]{1,0:T(8,128)(2,1)S(1)} %fusion.144), channel_id=1, source_target_pairs={{0,2},{1,3},{2,6},{3,7},{4,0},{5,1},{6,10},{7,11},{8,4},{9,5},{10,... | collective-permute-start | bytes 393224 | tf_op jit(solution)/shard_map/ppermute | solution.py:365
  211.2 6.1 %collective-permute-start.11 = (f16[64,1024]{1,0:T(8,128)(2,1)S(1)}, f16[64,1024]{1,0:T(8,128)(2,1)S(1)}, u32[]{:S(2)}, u32[]{:S(2)}) collective-permute-start(f16[64,1024]{1,0:T(8,128)(2,1)S(1)} %fusion.151), channel_id=1, source_target_pairs={{0,4},{1,5},{2,0},{3,1},{4,8},{5,9},{6,2},{7,3},{8,12},{9,13},{10,... | collective-permute-start | bytes 393224 | tf_op jit(solution)/shard_map/ppermute | solution.py:365
  213.4 6.1 %collective-permute-start.37 = (f16[64,1024]{1,0:T(8,128)(2,1)S(1)}, f16[64,1024]{1,0:T(8,128)(2,1)S(1)}, u32[]{:S(2)}, u32[]{:S(2)}) collective-permute-start(f16[64,1024]{1,0:T(8,128)(2,1)S(1)} %fusion.129), channel_id=1, source_target_pairs={{0,2},{1,3},{2,6},{3,7},{4,0},{5,1},{6,10},{7,11},{8,4},{9,5},{10,... | collective-permute-start | bytes 393224 | tf_op jit(solution)/shard_map/ppermute | solution.py:365
  214.3 6.1 %collective-permute-start.28 = (f16[64,1024]{1,0:T(8,128)(2,1)S(1)}, f16[64,1024]{1,0:T(8,128)(2,1)S(1)}, u32[]{:S(2)}, u32[]{:S(2)}) collective-permute-start(f16[64,1024]{1,0:T(8,128)(2,1)S(1)} %fusion.136), channel_id=1, source_target_pairs={{0,4},{1,5},{2,0},{3,1},{4,8},{5,9},{6,2},{7,3},{8,12},{9,13},{10,... | collective-permute-start | bytes 393224 | tf_op jit(solution)/shard_map/ppermute | solution.py:365
  216.5 6.0 %collective-permute-start.20 = (f16[64,1024]{1,0:T(8,128)(2,1)S(1)}, f16[64,1024]{1,0:T(8,128)(2,1)S(1)}, u32[]{:S(2)}, u32[]{:S(2)}) collective-permute-start(f16[64,1024]{1,0:T(8,128)(2,1)S(1)} %fusion.143), channel_id=1, source_target_pairs={{0,2},{1,3},{2,6},{3,7},{4,0},{5,1},{6,10},{7,11},{8,4},{9,5},{10,... | collective-permute-start | bytes 393224 | tf_op jit(solution)/shard_map/ppermute | solution.py:365
  217.3 5.3 %collective-permute-start.12 = (f16[64,1024]{1,0:T(8,128)(2,1)S(1)}, f16[64,1024]{1,0:T(8,128)(2,1)S(1)}, u32[]{:S(2)}, u32[]{:S(2)}) collective-permute-start(f16[64,1024]{1,0:T(8,128)(2,1)S(1)} %fusion.150), channel_id=1, source_target_pairs={{0,4},{1,5},{2,0},{3,1},{4,8},{5,9},{6,2},{7,3},{8,12},{9,13},{10,... | collective-permute-start | bytes 393224 | tf_op jit(solution)/shard_map/ppermute | solution.py:365
  219.6 5.1 %collective-permute-start.38 = (f16[64,1024]{1,0:T(8,128)(2,1)S(1)}, f16[64,1024]{1,0:T(8,128)(2,1)S(1)}, u32[]{:S(2)}, u32[]{:S(2)}) collective-permute-start(f16[64,1024]{1,0:T(8,128)(2,1)S(1)} %fusion.128), channel_id=1, source_target_pairs={{0,2},{1,3},{2,6},{3,7},{4,0},{5,1},{6,10},{7,11},{8,4},{9,5},{10,... | collective-permute-start | bytes 393224 | tf_op jit(solution)/shard_map/ppermute | solution.py:365
  220.4 7.2 %collective-permute-start.29 = (f16[64,1024]{1,0:T(8,128)(2,1)S(1)}, f16[64,1024]{1,0:T(8,128)(2,1)S(1)}, u32[]{:S(2)}, u32[]{:S(2)}) collective-permute-start(f16[64,1024]{1,0:T(8,128)(2,1)S(1)} %fusion.135), channel_id=1, source_target_pairs={{0,4},{1,5},{2,0},{3,1},{4,8},{5,9},{6,2},{7,3},{8,12},{9,13},{10,... | collective-permute-start | bytes 393224 | tf_op jit(solution)/shard_map/ppermute | solution.py:365
  222.5 5.0 %collective-permute-start.21 = (f16[64,1024]{1,0:T(8,128)(2,1)S(1)}, f16[64,1024]{1,0:T(8,128)(2,1)S(1)}, u32[]{:S(2)}, u32[]{:S(2)}) collective-permute-start(f16[64,1024]{1,0:T(8,128)(2,1)S(1)} %fusion.142), channel_id=1, source_target_pairs={{0,2},{1,3},{2,6},{3,7},{4,0},{5,1},{6,10},{7,11},{8,4},{9,5},{10,... | collective-permute-start | bytes 393224 | tf_op jit(solution)/shard_map/ppermute | solution.py:365
  222.7 5.0 %collective-permute-start.13 = (f16[64,1024]{1,0:T(8,128)(2,1)S(1)}, f16[64,1024]{1,0:T(8,128)(2,1)S(1)}, u32[]{:S(2)}, u32[]{:S(2)}) collective-permute-start(f16[64,1024]{1,0:T(8,128)(2,1)S(1)} %fusion.149), channel_id=1, source_target_pairs={{0,4},{1,5},{2,0},{3,1},{4,8},{5,9},{6,2},{7,3},{8,12},{9,13},{10,... | collective-permute-start | bytes 393224 | tf_op jit(solution)/shard_map/ppermute | solution.py:365

commit v2 on v1

--- a/solution.py
+++ b/solution.py
@@ -346,26 +346,44 @@
     return jnp.max(jnp.abs(values)).astype(jnp.float32)
 
 
-def reduce_ring(terms, scale, forward, devices, position):
-    chips = devices // 2
-    core = position % 2
-    place = ring_place(position // 2, chips)
-    step_by = 1 if forward else -1
-    route = []
-    for device in range(devices):
-        ahead = ring_chip((ring_place(device // 2, chips) + step_by) % chips, chips)
-        route.append((device, ahead * 2 + device % 2))
-
-    def term(distance):
-        chip = ring_chip((place + step_by * distance + 2 * chips) % chips, chips)
-        return lax.dynamic_index_in_dim(terms, chip, 0, keepdims=False) * scale
-
-    moving = term(-1).astype(jnp.float16)
-    for step in range(chips - 1):
-        moving = lax.ppermute(moving, "lon", route).astype(jnp.float32) + term(-2 - step)
-        if step < chips - 2:
-            moving = moving.astype(jnp.float16)
-    return moving / scale
+class Ring:
+    def __init__(self, terms, scale, forward, devices, position):
+        self.chips = devices // 2
+        self.terms, self.scale = terms, scale
+        self.place = ring_place(position // 2, self.chips)
+        self.ahead = 1 if forward else -1
+        self.route = []
+        for device in range(devices):
+            peer = ring_chip(
+                (ring_place(device // 2, self.chips) + self.ahead) % self.chips, self.chips
+            )
+            self.route.append((device, peer * 2 + device % 2))
+
+    def term(self, distance):
+        chip = ring_chip(
+            (self.place + self.ahead * distance + 2 * self.chips) % self.chips, self.chips
+        )
+        return lax.dynamic_index_in_dim(self.terms, chip, 0, keepdims=False) * self.scale
+
+    def first(self):
+        return self.term(-1).astype(jnp.float16)
+
+    def step(self, moving, step):
+        moving = lax.ppermute(moving, "lon", self.route).astype(jnp.float32)
+        moving = moving + self.term(-2 - step)
+        return moving.astype(jnp.float16) if step < self.chips - 2 else moving / self.scale
+
+
+def rings_beside(rings, stages, value):
+    moving = [ring.first() for ring in rings]
+    steps = rings[0].chips - 1
+    for step in range(max(steps, len(stages))):
+        moving, value = lax.optimization_barrier((moving, value))
+        if step < steps:
+            moving = [ring.step(block, step) for ring, block in zip(rings, moving)]
+        if step < len(stages):
+            value = stages[step](value)
+    return moving, value
 
 
 def per_device(
@@ -441,39 +459,62 @@
     normed_rows = split_rows(normed)
     attended_rows = split_rows(attended)
     rights = [grad_packed[:, i * model : (i + 1) * model] for i in range(3)] + [grad_flat]
-    reduced = []
+    rings = []
     for lane, right in enumerate(rights):
         rows = normed_rows if lane < 3 else attended_rows
         far = lax.ppermute(right, "lon", pairs)
         terms = (dot32(rows[0], right) + dot32(rows[1], far)).reshape(chips, -1, model)
-        reduced.append(reduce_ring(terms, scale, lane % 2 == 0, devices, position))
+        rings.append(Ring(terms, scale, lane % 2 == 0, devices, position))
+
+    fluxes = flux_weight.shape[1]
+    reach = KERNEL // 2
+
+    def update(values):
+        attended, shifted = values
+        change = dot32(attended, full_output)
+        updated = from_windows(
+            (shifted.astype(jnp.float32) + change).astype(jnp.bfloat16), height, width, WIN
+        )
+        moved = from_behind(updated[:, width - shift :], "lon", 1)
+        return jnp.concatenate([moved, updated[:, : width - shift]], axis=1)
+
+    def regrid(atmosphere_out):
+        flux = dot32(atmosphere_out.reshape(tokens, model), flux_weight).astype(jnp.bfloat16)
+        pieces = jnp.einsum("cf,kcd->kfd", flux, blocks, preferred_element_type=jnp.float32)
+        return atmosphere_out, pieces.reshape(2 * fluxes, tokens)
+
+    def force(values):
+        atmosphere_out, pieces = values
+        every = small_gather(pieces, devices, 2).reshape(devices, 2, fluxes, tokens)
+        here = (regrid_target == position)[:, :, None, None]
+        arrived = jnp.sum(jnp.where(here, every, 0.0), axis=(0, 1))
+        forcing = jnp.dot(arrived.T, flux_embed, precision=HIGHEST).reshape(
+            height, width, channels
+        )
+        return atmosphere_out, (ocean_state.astype(jnp.float32) + forcing).astype(jnp.bfloat16)
+
+    def convolve(values):
+        atmosphere_out, forced = values
+        margin = extended(forced, (("lon", 1),), reach)
+        padded = jnp.pad(margin.astype(jnp.float32), ((reach, reach), (0, 0), (0, 0)))
+        conv = depthwise_conv(padded, depthwise, height, width)
+        ocean_normed = layer_norm(conv, ocean_gain).astype(jnp.bfloat16)
+        return atmosphere_out, ocean_normed.reshape(tokens, channels)
+
+    def advance(values):
+        atmosphere_out, ocean_normed = values
+        hidden = jax.nn.gelu(dot32(ocean_normed, expand)).astype(jnp.bfloat16)
+        ocean_change = dot32(hidden, contract).reshape(height, width, channels)
+        ocean_next = (
+            ocean_state.astype(jnp.float32)
+            + ocean_mask.astype(jnp.float32)[..., None] * ocean_change
+        ).astype(jnp.bfloat16)
+        return atmosphere_out, ocean_next
+
+    reduced, (atmosphere_out, ocean_next) = rings_beside(
+        rings, (update, regrid, force, convolve, advance), (attended, shifted)
+    )
     weight_grad = jnp.concatenate(reduced, axis=1)
-
-    change = dot32(attended, full_output)
-    updated = from_windows(
-        (shifted.astype(jnp.float32) + change).astype(jnp.bfloat16), height, width, WIN
-    )
-    moved = from_behind(updated[:, width - shift :], "lon", 1)
-    atmosphere_out = jnp.concatenate([moved, updated[:, : width - shift]], axis=1)
-    flux = dot32(atmosphere_out.reshape(tokens, model), flux_weight).astype(jnp.bfloat16)
-    pieces = jnp.einsum("cf,kcd->kfd", flux, blocks, preferred_element_type=jnp.float32)
-    fluxes = flux_weight.shape[1]
-    every = small_gather(pieces.reshape(2 * fluxes, tokens), devices, 2)
-    every = every.reshape(devices, 2, fluxes, tokens)
-    here = (regrid_target == position)[:, :, None, None]
-    arrived = jnp.sum(jnp.where(here, every, 0.0), axis=(0, 1))
-    forcing = jnp.dot(arrived.T, flux_embed, precision=HIGHEST).reshape(height, width, channels)
-    forced = (ocean_state.astype(jnp.float32) + forcing).astype(jnp.bfloat16)
-    reach = KERNEL // 2
-    margin = extended(forced, (("lon", 1),), reach)
-    padded = jnp.pad(margin.astype(jnp.float32), ((reach, reach), (0, 0), (0, 0)))
-    conv = depthwise_conv(padded, depthwise, height, width)
-    ocean_normed = layer_norm(conv, ocean_gain).astype(jnp.bfloat16)
-    hidden = jax.nn.gelu(dot32(ocean_normed.reshape(tokens, channels), expand)).astype(jnp.bfloat16)
-    ocean_change = dot32(hidden, contract).reshape(height, width, channels)
-    ocean_next = (
-        ocean_state.astype(jnp.float32) + ocean_mask.astype(jnp.float32)[..., None] * ocean_change
-    ).astype(jnp.bfloat16)
     return (atmosphere_out, ocean_next, weight_grad)
 
 

time: 230 us -> 247 us (1.074)
  other arithmetic: 19.2 us -> 48.8 us
  waiting for transfers between devices: 14.6 us -> 9.25 us
  starting transfers between devices: 39.4 us -> 36.8 us
    convert_element_type x33 -> x32, other arithmetic: 3.42 us -> 29.9 us  [the longest x24 25.9 us: step(): moving.astype(jnp.float16)]
    div x4, other arithmetic: 0.18 us -> 3.98 us  [step(): moving / self.scale]
    ppermute x28, waiting for transfers between devices: 11.2 us -> 7.51 us  [step(): moving = lax.ppermute(moving, 'lon', self.route).astype(jnp.float32)]
    ppermute x1, waiting for transfers between devices: 3.29 us -> 0.5 us  [extended(): before = lax.ppermute(last, axis, up)]
  transfers between devices with their start and end apart: 39 -> 39, of which waited for: 22 -> 9; matrix products, arithmetic and copies ran while one was open for 26% -> 22% of each run, Pallas kernels for 15% -> 7%
where the time goes in v2:
time: 247 us; the launch traced here: 245 us
  Pallas kernels  98 us (40%)
  other arithmetic  48.8 us (20%)
  starting transfers between devices  36.8 us (15%)
  matrix products  29.9 us (12%)
  local copies, waits for them, and re-layouts  17.7 us (7%)
  waiting for transfers between devices  9.25 us (4%)
  between operations  5.07 us (2%)
    pallas_call x1, Pallas kernels, gather_weights(): pl.pallas_call(functools.partial(gather_weights_kernel, n), out_shape=(ja...  66.4 us
    ppermute x28, starting transfers between devices, step(): moving = lax.ppermute(moving, 'lon', self.route).astype(jnp.float32)  28.7 us
    convert_element_type x24, other arithmetic, step(): moving.astype(jnp.float16)  25.9 us
    dot_general x12, matrix products, dot32(): return jnp.dot(left, right, preferred_element_type=jnp.float32)  25.1 us
    pallas_call x2, Pallas kernels, small_gather(): pl.pallas_call(functools.partial(small_gather_kernel, n), out_shape=jax.S...  16.1 us
    pallas_call x1, Pallas kernels, attention(): pl.pallas_call(attention_kernel, grid=(tokens // cells,), out_shape=(jax....  15.4 us
    ppermute x28, waiting for transfers between devices, step(): moving = lax.ppermute(moving, 'lon', self.route).astype(jnp.float32)  7.51 us
    reduce_sum x2, other arithmetic, layer_norm(): center = values - jnp.mean(values, axis=-1, keepdims=True)  4.95 us
  transfers between devices with their start and end apart: 39, of which 9 were waited for; matrix products, arithmetic and copies ran while one was open for 22% of the time, Pallas kernels for 7%

profile of v2, /device:TPU:0, one launch (start us, length us, event | category | flops | bytes accessed | tf_op | source)
XLA Modules:
  0.0 245.5 jit_solution(15278809126438456923)
XLA Ops:
  0.7 1.0 fusion.166
  2.4 1.1 fusion.188
  4.1 66.4 %shard_map.184 = (bf16[1024,4096]{1,0:T(8,128)(2,1)}, f32[16,8,256]{2,1,0:T(8,128)}) custom-call(bf16[64,3072]{1,0:T(8,128)(2,1)} %proj_ref.1, bf16[64,1024]{1,0:T(8,128)(2,1)} %out_weight_ref.1, f32[8,256]{1,0:T(8,128)} %broadcast_in_dim.45.surface_ref), custom_call_target="tpu_custom_call" | custom-call | tf_op jit(solution)/shard_map/pallas_call | solution.py:230
  72.2 1.3 fusion.157
  73.4 1.2 add_convert_fusion
  74.7 2.5 %collective-permute-start = (bf16[8,4,1024]{2,1,0:T(4,128)(2,1)S(1)}, bf16[8,4,1024]{2,1,0:T(4,128)(2,1)S(1)}, u32[]{:S(2)}, u32[]{:S(2)}) collective-permute-start(bf16[8,4,1024]{2,1,0:T(4,128)(2,1)S(1)} %slice.462), channel_id=1, source_target_pairs={{1,0},{2,1},{3,2},{4,3},{5,4},{6,5},{7,6},{8,7},{9,8},{10,9},{11,1... | collective-permute-start | bytes 196616 | tf_op jit(solution)/shard_map/ppermute | solution.py:25
  82.9 4.8 %fusion.2.packed_ref = bf16[256,3072]{1,0:T(8,128)(2,1)S(1)} fusion(bf16[256,1024]{1,0:T(8,128)(2,1)S(1)} %multiply_convert_fusion, bf16[1024,4096]{1,0:T(8,128)(2,1)} %get-tuple-element.49), kind=kOutput, calls=%fused_computation.45 | convolution fusion | flops 1611399168 | bytes 8388608 | tf_op jit(solution)/shard_map/dot_general | solution.py:342
  87.7 2.5 %fusion.20.grad_ref = bf16[256,1024]{1,0:T(8,128)(2,1)S(1)} fusion(bf16[256,1024]{1,0:T(8,128)(2,1)} %bitcast.17, bf16[1024,4096]{1,0:T(8,128)(2,1)} %get-tuple-element.49), kind=kOutput, calls=%fused_computation.67 | convolution fusion | flops 537133056 | bytes 3145728 | tf_op jit(solution)/shard_map/dot_general | solution.py:439
  90.2 15.4 %shard_map.185 = (bf16[256,1024]{1,0:T(8,128)(2,1)S(1)}, bf16[256,3072]{1,0:T(8,128)(2,1)S(1)}) custom-call(bf16[256,3072]{1,0:T(8,128)(2,1)S(1)} %fusion.2.packed_ref, bf16[256,1024]{1,0:T(8,128)(2,1)S(1)} %fusion.20.grad_ref), custom_call_target="tpu_custom_call" | custom-call | flops 939524096 | bytes 4194304 | tf_op jit(solution)/shard_map/pallas_call | solution.py:312
  105.6 1.2 fusion.181
  108.4 1.0 copy.39
  109.4 2.0 copy.37
  111.4 2.2 constant_dynamic-slice_fusion
  113.6 1.8 fusion.177
  115.4 1.8 fusion.175
  122.0 8.0 %shard_map.186 = f32[16,8,128]{2,1,0:T(8,128)} custom-call(f32[8,128]{1,0:T(8,128)} %broadcast_in_dim.47.x_ref), custom_call_target="tpu_custom_call" | custom-call | tf_op jit(solution)/shard_map/pallas_call | solution.py:115
  130.0 1.5 slice_reduce_fusion
  132.7 1.5 fusion.173
  134.2 1.7 fusion.189
  136.1 1.7 convolution_add_fusion.3
  137.8 2.1 convolution_add_fusion.2
  140.0 1.6 convolution_add_fusion.1
  143.2 1.5 convolution_add_fusion
  145.5 2.3 fusion.23
  148.4 1.2 collective-permute-start.8
  151.3 1.0 collective-permute-start.10
  153.3 1.2 collective-permute-done.12
  156.2 1.2 fusion.155
  157.4 1.2 collective-permute-done.10
  159.6 1.0 fusion.154
  160.7 1.7 fusion.152
  162.7 1.7 collective-permute-start.14
  164.7 1.7 collective-permute-start.16
  167.5 1.3 collective-permute-done.13
  168.8 1.0 fusion.151
  169.8 1.0 collective-permute-done.15
  170.9 1.0 fusion.149
  171.9 1.0 fusion.150
  173.0 1.0 fusion.148
  174.4 1.7 collective-permute-start.18
  176.4 1.7 collective-permute-start.20
  178.1 8.2 %shard_map.187 = f32[16,8,256]{2,1,0:T(8,128)} custom-call(f32[8,256]{1,0:T(8,128)} %reshape.270.x_ref), custom_call_target="tpu_custom_call" | custom-call | tf_op jit(solution)/shard_map/pallas_call | solution.py:115
  189.1 1.0 fusion.145
  191.2 1.0 fusion.144
  192.2 3.4 %collective-permute-start.26 = (bf16[8,3,512]{2,1,0:T(4,128)(2,1)S(1)}, bf16[8,3,512]{2,1,0:T(4,128)(2,1)S(1)}, u32[]{:S(2)}, u32[]{:S(2)}) collective-permute-start(bf16[8,3,512]{2,1,0:T(4,128)(2,1)S(1)} %get-tuple-element.105), channel_id=1, source_target_pairs={{1,0},{2,1},{3,2},{4,3},{5,4},{6,5},{7,6},{8,7},{9,8},{10,9},{11,1... | collective-permute-start | bytes 73736 | tf_op jit(solution)/shard_map/ppermute | solution.py:36
  197.5 2.0 collective-permute-start.22
  199.5 2.0 collective-permute-start.24
  202.2 4.8 %fusion.179 = (f32[8,32]{1,0:T(8,128)S(1)}, f32[8,32,512]{2,1,0:T(8,128)S(1)}) fusion(f32[512]{0:T(512)S(1)} %bitcast.365, f32[512]{0:T(512)S(1)} %bitcast.366, f32[512]{0:T(512)S(1)} %bitcast.319, f32[512]{0:T(512)S(1)} %bitcast.320, f32[512]{0:T(512)} %bitcast.321, f32[512]{0:T(512)} %bitcast.322, f32[512]{0:T(512)} %bitcast.323, f32[512]{0:T(512)} %bitcast.324, ...), kind=kLoop, calls=%fused_computation.295 | loop fusion | flops 12844800 | bytes 4951040 | tf_op jit(solution)/shard_map/reduce_sum | solution.py:42
  208.4 1.7 fusion.141
  212.1 2.0 collective-permute-start.28
  214.2 2.0 collective-permute-start.30
  216.1 3.2 %fusion.33 = f32[256,512]{1,0:T(8,128)S(1)} fusion(bf16[2048,512]{1,0:T(8,128)(2,1)S(1)} %copy-done, bf16[256,512]{1,0:T(8,128)(2,1)S(1)} %bitcast.314, bf16[512,2048]{1,0:T(8,128)(2,1)} %param.30), kind=kOutput, calls=%fused_computation.82 | convolution fusion | flops 1078460416 | bytes 4980736 | tf_op jit(solution)/shard_map/dot_general | solution.py:342
  220.1 1.0 fusion.139
  221.2 1.0 fusion.137
  222.2 1.0 fusion.138
  223.3 1.0 fusion.136
  224.5 1.9 collective-permute-start.32
  226.5 1.9 collective-permute-start.34
  230.3 1.0 collective-permute-done.33
  232.4 1.0 fusion.134
  234.5 1.9 collective-permute-start.37
  236.6 1.9 collective-permute-start.35
  240.4 1.0 collective-permute-done.36
  244.4 1.0 pad_maximum_fusion
  (182 shorter events, 43.4 us)
Async XLA Ops:
  0.6 215.5 %copy-start = (bf16[2048,512]{1,0:T(8,128)(2,1)S(1)}, bf16[2048,512]{1,0:T(8,128)(2,1)}, u32[]{:S(2)}) copy-start(bf16[2048,512]{1,0:T(8,128)(2,1)} %param.31) | copy-start | bytes 6291460
  0.6 77.7 %copy-start.17 = (f32[7,7,512]{2,1,0:T(8,128)S(1)}, f32[7,7,512]{2,1,0:T(8,128)}, u32[]{:S(2)}) copy-start(f32[7,7,512]{2,1,0:T(8,128)} %param.28) | copy-start | bytes 301060
  72.1 7.7 %copy-start.14 = (bf16[8,32,1024]{2,1,0:T(8,128)(2,1)S(1)}, bf16[8,32,1024]{2,1,0:T(8,128)(2,1)}, u32[]{:S(2)}) copy-start(bf16[8,32,1024]{2,1,0:T(8,128)(2,1)} %param.18) | copy-start | bytes 1572868
  74.7 5.4 %collective-permute-start = (bf16[8,4,1024]{2,1,0:T(4,128)(2,1)S(1)}, bf16[8,4,1024]{2,1,0:T(4,128)(2,1)S(1)}, u32[]{:S(2)}, u32[]{:S(2)}) collective-permute-start(bf16[8,4,1024]{2,1,0:T(4,128)(2,1)S(1)} %slice.462), channel_id=1, source_target_pairs={{1,0},{2,1},{3,2},{4,3},{5,4},{6,5},{7,6},{8,7},{9,8},{10,9},{11,1... | collective-permute-start | bytes 196616 | tf_op jit(solution)/shard_map/ppermute | solution.py:25
  78.1 2.9 %collective-permute-start.1 = (bf16[8,4,1024]{2,1,0:T(4,128)(2,1)S(1)}, bf16[8,4,1024]{2,1,0:T(4,128)(2,1)S(1)}, u32[]{:S(2)}, u32[]{:S(2)}) collective-permute-start(bf16[8,4,1024]{2,1,0:T(4,128)(2,1)S(1)} %slice.351), channel_id=1, source_target_pairs={{1,0},{2,1},{3,2},{4,3},{5,4},{6,5},{7,6},{8,7},{9,8},{10,9},{11,1... | collective-permute-start | bytes 196616 | tf_op jit(solution)/shard_map/ppermute | solution.py:25
  81.0 1.9 copy-start.11
  82.9 4.8 %copy-start.13 = (bf16[256,1024]{1,0:T(8,128)(2,1)}, bf16[256,1024]{1,0:T(8,128)(2,1)S(1)}, u32[]{:S(2)}) copy-start(bf16[256,1024]{1,0:T(8,128)(2,1)S(1)} %multiply_convert_fusion) | copy-start | bytes 1572868
  105.6 2.0 copy-start.1
  111.4 2.2 copy-start.2
  117.2 25.9 %collective-permute-start.7 = (bf16[256,1024]{1,0:T(8,128)(2,1)}, bf16[256,1024]{1,0:T(8,128)(2,1)}, u32[]{:S(2)}, u32[]{:S(2)}) collective-permute-start(bf16[256,1024]{1,0:T(8,128)(2,1)} %bitcast.17), channel_id=1, source_target_pairs={{0,1},{1,0},{2,3},{3,2},{4,5},{5,4},{6,7},{7,6},{8,9},{9,8},{10,11... | collective-permute-start | bytes 1572872 | tf_op jit(solution)/shard_map/ppermute | solution.py:465
  117.6 18.3 %collective-permute-start.2 = (bf16[512,256]{1,0:T(8,128)(2,1)}, bf16[512,256]{1,0:T(8,128)(2,1)}, u32[]{:S(2)}, u32[]{:S(2)}) collective-permute-start(bf16[512,256]{1,0:T(8,128)(2,1)} %bitcast.18), channel_id=1, source_target_pairs={{0,1},{1,0},{2,3},{3,2},{4,5},{5,4},{6,7},{7,6},{8,9},{9,8},{10,11... | collective-permute-start | bytes 786440 | tf_op jit(solution)/shard_map/ppermute | solution.py:457
  117.7 18.4 %collective-permute-start.3 = (bf16[256,1024]{1,0:T(8,128)(2,1)}, bf16[256,1024]{1,0:T(8,128)(2,1)}, u32[]{:S(2)}, u32[]{:S(2)}) collective-permute-start(bf16[256,1024]{1,0:T(8,128)(2,1)} %get-tuple-element.99), channel_id=1, source_target_pairs={{0,1},{1,0},{2,3},{3,2},{4,5},{5,4},{6,7},{7,6},{8,9},{9,8},{10,11... | collective-permute-start | bytes 1572872 | tf_op jit(solution)/shard_map/ppermute | solution.py:465
  131.5 6.3 %collective-permute-start.4 = (bf16[256,1024]{1,0:T(8,128)(2,1)}, bf16[256,1024]{1,0:T(8,128)(2,1)}, u32[]{:S(2)}, u32[]{:S(2)}) collective-permute-start(bf16[256,1024]{1,0:T(8,128)(2,1)} %get-tuple-element.98), channel_id=1, source_target_pairs={{0,1},{1,0},{2,3},{3,2},{4,5},{5,4},{6,7},{7,6},{8,9},{9,8},{10,11... | collective-permute-start | bytes 1572872 | tf_op jit(solution)/shard_map/ppermute | solution.py:465
  131.6 8.4 %collective-permute-start.5 = (bf16[256,1024]{1,0:T(8,128)(2,1)}, bf16[256,1024]{1,0:T(8,128)(2,1)S(1)}, u32[]{:S(2)}, u32[]{:S(2)}) collective-permute-start(bf16[256,1024]{1,0:T(8,128)(2,1)} %get-tuple-element.97), channel_id=1, source_target_pairs={{0,1},{1,0},{2,3},{3,2},{4,5},{5,4},{6,7},{7,6},{8,9},{9,8},{10,11... | collective-permute-start | bytes 1572872 | tf_op jit(solution)/shard_map/ppermute | solution.py:465
  134.2 1.9 copy-start.8
  135.9 1.9 copy-start.7
  136.0 7.2 %collective-permute-start.6 = (bf16[512,256]{1,0:T(8,128)(2,1)S(1)}, bf16[512,256]{1,0:T(8,128)(2,1)S(1)}, u32[]{:S(2)}, u32[]{:S(2)}) collective-permute-start(bf16[512,256]{1,0:T(8,128)(2,1)S(1)} %bitcast.315), channel_id=1, source_target_pairs={{0,1},{1,0},{2,3},{3,2},{4,5},{5,4},{6,7},{7,6},{8,9},{9,8},{10,11... | collective-permute-start | bytes 786440 | tf_op jit(solution)/shard_map/ppermute | solution.py:457
  137.8 3.8 %copy-start.3 = (f32[512,1024]{1,0:T(8,128)}, f32[512,1024]{1,0:T(8,128)S(1)}, u32[]{:S(2)}) copy-start(f32[512,1024]{1,0:T(8,128)S(1)} %convolution_add_fusion.3) | copy-start | bytes 6291460
  140.0 3.1 %copy-start.5 = (f32[512,1024]{1,0:T(8,128)}, f32[512,1024]{1,0:T(8,128)S(1)}, u32[]{:S(2)}) copy-start(f32[512,1024]{1,0:T(8,128)S(1)} %convolution_add_fusion.2) | copy-start | bytes 6291460
  141.6 3.1 %copy-start.4 = (f32[512,1024]{1,0:T(8,128)}, f32[512,1024]{1,0:T(8,128)S(1)}, u32[]{:S(2)}) copy-start(f32[512,1024]{1,0:T(8,128)S(1)} %convolution_add_fusion.1) | copy-start | bytes 6291460
  143.1 2.4 copy-start.12
  144.7 3.1 %copy-start.6 = (f32[512,1024]{1,0:T(8,128)}, f32[512,1024]{1,0:T(8,128)S(1)}, u32[]{:S(2)}) copy-start(f32[512,1024]{1,0:T(8,128)S(1)} %convolution_add_fusion) | copy-start | bytes 6291460
  145.5 2.9 %copy-start.26 = (s32[16,2]{0,1:T(2,128)S(1)}, s32[16,2]{0,1:T(2,128)}, u32[]{:S(2)}) copy-start(s32[16,2]{0,1:T(2,128)} %param.33) | copy-start | bytes 388
  147.9 18.5 %copy-start.15 = (bf16[1,2,256,256]{3,2,1,0:T(8,128)(2,1)S(1)}, bf16[1,2,256,256]{3,2,1,0:T(8,128)(2,1)}, u32[]{:S(2)}) copy-start(bf16[1,2,256,256]{3,2,1,0:T(8,128)(2,1)} %param.32) | copy-start | bytes 786436
  147.9 18.5 %copy-start.20 = (bf16[1024,4]{0,1:T(4,128)(2,1)S(1)}, bf16[1024,4]{0,1:T(4,128)(2,1)}, u32[]{:S(2)}) copy-start(bf16[1024,4]{0,1:T(4,128)(2,1)} %param.26) | copy-start | bytes 24580
  147.9 6.6 %collective-permute-start.12 = (bf16[8,4,1024]{2,1,0:T(4,128)(2,1)S(1)}, bf16[8,4,1024]{2,1,0:T(4,128)(2,1)S(1)}, u32[]{:S(2)}, u32[]{:S(2)}) collective-permute-start(bf16[8,4,1024]{2,1,0:T(4,128)(2,1)S(1)} %slice.463), channel_id=1, source_target_pairs={{15,0},{0,1},{1,2},{2,3},{3,4},{4,5},{5,6},{6,7},{7,8},{8,9},{9,10... | collective-permute-start | bytes 196616 | tf_op jit(solution)/shard_map/ppermute | solution.py:25
  148.4 7.8 %collective-permute-start.8 = (f16[64,1024]{1,0:T(8,128)(2,1)}, f16[64,1024]{1,0:T(8,128)(2,1)}, u32[]{:S(2)}, u32[]{:S(2)}) collective-permute-start(f16[64,1024]{1,0:T(8,128)(2,1)} %fusion.159), channel_id=1, source_target_pairs={{0,4},{1,5},{2,0},{3,1},{4,8},{5,9},{6,2},{7,3},{8,12},{9,13},{10,... | collective-permute-start | bytes 393224 | tf_op jit(solution)/shard_map/ppermute | solution.py:372
  150.3 9.3 %collective-permute-start.9 = (f16[64,1024]{1,0:T(8,128)(2,1)S(1)}, f16[64,1024]{1,0:T(8,128)(2,1)S(1)}, u32[]{:S(2)}, u32[]{:S(2)}) collective-permute-start(f16[64,1024]{1,0:T(8,128)(2,1)S(1)} %fusion.160), channel_id=1, source_target_pairs={{0,2},{1,3},{2,6},{3,7},{4,0},{5,1},{6,10},{7,11},{8,4},{9,5},{10,... | collective-permute-start | bytes 393224 | tf_op jit(solution)/shard_map/ppermute | solution.py:372
  151.3 7.3 %collective-permute-start.10 = (f16[64,1024]{1,0:T(8,128)(2,1)}, f16[64,1024]{1,0:T(8,128)(2,1)S(1)}, u32[]{:S(2)}, u32[]{:S(2)}) collective-permute-start(f16[64,1024]{1,0:T(8,128)(2,1)} %fusion.161), channel_id=1, source_target_pairs={{0,4},{1,5},{2,0},{3,1},{4,8},{5,9},{6,2},{7,3},{8,12},{9,13},{10,... | collective-permute-start | bytes 393224 | tf_op jit(solution)/shard_map/ppermute | solution.py:372
  152.3 8.4 %collective-permute-start.11 = (f16[64,1024]{1,0:T(8,128)(2,1)}, f16[64,1024]{1,0:T(8,128)(2,1)S(1)}, u32[]{:S(2)}, u32[]{:S(2)}) collective-permute-start(f16[64,1024]{1,0:T(8,128)(2,1)} %fusion.162), channel_id=1, source_target_pairs={{0,2},{1,3},{2,6},{3,7},{4,0},{5,1},{6,10},{7,11},{8,4},{9,5},{10,... | collective-permute-start | bytes 393224 | tf_op jit(solution)/shard_map/ppermute | solution.py:372
  156.2 16.8 %copy-start.10 = (bf16[8,32,1024]{2,1,0:T(8,128)(2,1)}, bf16[8,32,1024]{2,1,0:T(8,128)(2,1)S(1)}, u32[]{:S(2)}) copy-start(bf16[8,32,1024]{2,1,0:T(8,128)(2,1)S(1)} %pad_maximum_fusion.1) | copy-start | bytes 1572868
  159.6 27.8 %copy-start.9 = (bf16[8,32,512]{2,1,0:T(8,128)(2,1)S(1)}, bf16[8,32,512]{2,1,0:T(8,128)(2,1)}, u32[]{:S(2)}) copy-start(bf16[8,32,512]{2,1,0:T(8,128)(2,1)} %param.19) | copy-start | bytes 786436
  162.3 6.4 %collective-permute-start.13 = (f16[64,1024]{1,0:T(8,128)(2,1)S(1)}, f16[64,1024]{1,0:T(8,128)(2,1)}, u32[]{:S(2)}, u32[]{:S(2)}) collective-permute-start(f16[64,1024]{1,0:T(8,128)(2,1)S(1)} %fusion.155), channel_id=1, source_target_pairs={{0,4},{1,5},{2,0},{3,1},{4,8},{5,9},{6,2},{7,3},{8,12},{9,13},{10,... | collective-permute-start | bytes 393224 | tf_op jit(solution)/shard_map/ppermute | solution.py:372
  162.7 9.2 %collective-permute-start.14 = (f16[64,1024]{1,0:T(8,128)(2,1)S(1)}, f16[64,1024]{1,0:T(8,128)(2,1)}, u32[]{:S(2)}, u32[]{:S(2)}) collective-permute-start(f16[64,1024]{1,0:T(8,128)(2,1)S(1)} %fusion.154), channel_id=1, source_target_pairs={{0,2},{1,3},{2,6},{3,7},{4,0},{5,1},{6,10},{7,11},{8,4},{9,5},{10,... | collective-permute-start | bytes 393224 | tf_op jit(solution)/shard_map/ppermute | solution.py:372
  164.4 6.5 %collective-permute-start.15 = (f16[64,1024]{1,0:T(8,128)(2,1)S(1)}, f16[64,1024]{1,0:T(8,128)(2,1)}, u32[]{:S(2)}, u32[]{:S(2)}) collective-permute-start(f16[64,1024]{1,0:T(8,128)(2,1)S(1)} %fusion.153), channel_id=1, source_target_pairs={{0,4},{1,5},{2,0},{3,1},{4,8},{5,9},{6,2},{7,3},{8,12},{9,13},{10,... | collective-permute-start | bytes 393224 | tf_op jit(solution)/shard_map/ppermute | solution.py:372
  164.7 8.2 %collective-permute-start.16 = (f16[64,1024]{1,0:T(8,128)(2,1)}, f16[64,1024]{1,0:T(8,128)(2,1)}, u32[]{:S(2)}, u32[]{:S(2)}) collective-permute-start(f16[64,1024]{1,0:T(8,128)(2,1)} %fusion.152), channel_id=1, source_target_pairs={{0,2},{1,3},{2,6},{3,7},{4,0},{5,1},{6,10},{7,11},{8,4},{9,5},{10,... | collective-permute-start | bytes 393224 | tf_op jit(solution)/shard_map/ppermute | solution.py:372
  166.9 20.5 %copy-start.21 = (f32[4,512]{1,0:T(4,128)S(1)}, f32[4,512]{1,0:T(4,128)}, u32[]{:S(2)}) copy-start(f32[4,512]{1,0:T(4,128)} %param.27) | copy-start | bytes 24580
  167.5 18.8 %copy-start.25 = (pred[16,8]{1,0:T(8,128)(4,1)S(1)}, pred[16,8]{1,0:T(8,128)(4,1)}, u32[]{:S(2)}) copy-start(pred[16,8]{1,0:T(8,128)(4,1)} %copy.41) | copy-start | bytes 388
  174.0 14.1 %collective-permute-start.17 = (f16[64,1024]{1,0:T(8,128)(2,1)S(1)}, f16[64,1024]{1,0:T(8,128)(2,1)S(1)}, u32[]{:S(2)}, u32[]{:S(2)}) collective-permute-start(f16[64,1024]{1,0:T(8,128)(2,1)S(1)} %fusion.151), channel_id=1, source_target_pairs={{0,4},{1,5},{2,0},{3,1},{4,8},{5,9},{6,2},{7,3},{8,12},{9,13},{10,... | collective-permute-start | bytes 393224 | tf_op jit(solution)/shard_map/ppermute | solution.py:372
  174.4 15.8 %collective-permute-start.18 = (f16[64,1024]{1,0:T(8,128)(2,1)S(1)}, f16[64,1024]{1,0:T(8,128)(2,1)S(1)}, u32[]{:S(2)}, u32[]{:S(2)}) collective-permute-start(f16[64,1024]{1,0:T(8,128)(2,1)S(1)} %fusion.150), channel_id=1, source_target_pairs={{0,2},{1,3},{2,6},{3,7},{4,0},{5,1},{6,10},{7,11},{8,4},{9,5},{10,... | collective-permute-start | bytes 393224 | tf_op jit(solution)/shard_map/ppermute | solution.py:372
  176.1 13.0 %collective-permute-start.19 = (f16[64,1024]{1,0:T(8,128)(2,1)S(1)}, f16[64,1024]{1,0:T(8,128)(2,1)}, u32[]{:S(2)}, u32[]{:S(2)}) collective-permute-start(f16[64,1024]{1,0:T(8,128)(2,1)S(1)} %fusion.149), channel_id=1, source_target_pairs={{0,4},{1,5},{2,0},{3,1},{4,8},{5,9},{6,2},{7,3},{8,12},{9,13},{10,... | collective-permute-start | bytes 393224 | tf_op jit(solution)/shard_map/ppermute | solution.py:372
  176.4 14.8 %collective-permute-start.20 = (f16[64,1024]{1,0:T(8,128)(2,1)S(1)}, f16[64,1024]{1,0:T(8,128)(2,1)}, u32[]{:S(2)}, u32[]{:S(2)}) collective-permute-start(f16[64,1024]{1,0:T(8,128)(2,1)S(1)} %fusion.148), channel_id=1, source_target_pairs={{0,2},{1,3},{2,6},{3,7},{4,0},{5,1},{6,10},{7,11},{8,4},{9,5},{10,... | collective-permute-start | bytes 393224 | tf_op jit(solution)/shard_map/ppermute | solution.py:372
  187.4 14.7 %copy-start.22 = (f32[1,1,512]{2,1,0:T(1,128)S(1)}, f32[1,1,512]{2,1,0:T(1,128)}, u32[]{:S(2)}) copy-start(f32[1,1,512]{2,1,0:T(1,128)} %get-tuple-element.106) | copy-start | bytes 6148
  188.1 14.1 %copy-start.23 = (f32[1,1,512]{2,1,0:T(1,128)S(1)}, f32[1,1,512]{2,1,0:T(1,128)}, u32[]{:S(2)}) copy-start(f32[1,1,512]{2,1,0:T(1,128)} %get-tuple-element.107) | copy-start | bytes 6148
  188.1 14.1 %copy-start.24 = (f32[1,1,512]{2,1,0:T(1,128)S(1)}, f32[1,1,512]{2,1,0:T(1,128)}, u32[]{:S(2)}) copy-start(f32[1,1,512]{2,1,0:T(1,128)} %get-tuple-element.108) | copy-start | bytes 6148
  192.2 7.2 %collective-permute-start.26 = (bf16[8,3,512]{2,1,0:T(4,128)(2,1)S(1)}, bf16[8,3,512]{2,1,0:T(4,128)(2,1)S(1)}, u32[]{:S(2)}, u32[]{:S(2)}) collective-permute-start(bf16[8,3,512]{2,1,0:T(4,128)(2,1)S(1)} %get-tuple-element.105), channel_id=1, source_target_pairs={{1,0},{2,1},{3,2},{4,3},{5,4},{6,5},{7,6},{8,7},{9,8},{10,9},{11,1... | collective-permute-start | bytes 73736 | tf_op jit(solution)/shard_map/ppermute | solution.py:36
  195.6 6.4 %collective-permute-start.25 = (bf16[8,3,512]{2,1,0:T(4,128)(2,1)S(1)}, bf16[8,3,512]{2,1,0:T(4,128)(2,1)S(1)}, u32[]{:S(2)}, u32[]{:S(2)}) collective-permute-start(bf16[8,3,512]{2,1,0:T(4,128)(2,1)S(1)} %get-tuple-element.104), channel_id=1, source_target_pairs={{0,1},{1,2},{2,3},{3,4},{4,5},{5,6},{6,7},{7,8},{8,9},{9,10},{10,1... | collective-permute-start | bytes 73736 | tf_op jit(solution)/shard_map/ppermute | solution.py:35
  197.5 9.9 %collective-permute-start.21 = (f16[64,1024]{1,0:T(8,128)(2,1)S(1)}, f16[64,1024]{1,0:T(8,128)(2,1)S(1)}, u32[]{:S(2)}, u32[]{:S(2)}) collective-permute-start(f16[64,1024]{1,0:T(8,128)(2,1)S(1)} %fusion.147), channel_id=1, source_target_pairs={{0,4},{1,5},{2,0},{3,1},{4,8},{5,9},{6,2},{7,3},{8,12},{9,13},{10,... | collective-permute-start | bytes 393224 | tf_op jit(solution)/shard_map/ppermute | solution.py:372
  197.5 12.5 %collective-permute-start.22 = (f16[64,1024]{1,0:T(8,128)(2,1)S(1)}, f16[64,1024]{1,0:T(8,128)(2,1)S(1)}, u32[]{:S(2)}, u32[]{:S(2)}) collective-permute-start(f16[64,1024]{1,0:T(8,128)(2,1)S(1)} %fusion.146), channel_id=1, source_target_pairs={{0,2},{1,3},{2,6},{3,7},{4,0},{5,1},{6,10},{7,11},{8,4},{9,5},{10,... | collective-permute-start | bytes 393224 | tf_op jit(solution)/shard_map/ppermute | solution.py:372
  199.5 8.9 %collective-permute-start.23 = (f16[64,1024]{1,0:T(8,128)(2,1)S(1)}, f16[64,1024]{1,0:T(8,128)(2,1)S(1)}, u32[]{:S(2)}, u32[]{:S(2)}) collective-permute-start(f16[64,1024]{1,0:T(8,128)(2,1)S(1)} %fusion.145), channel_id=1, source_target_pairs={{0,4},{1,5},{2,0},{3,1},{4,8},{5,9},{6,2},{7,3},{8,12},{9,13},{10,... | collective-permute-start | bytes 393224 | tf_op jit(solution)/shard_map/ppermute | solution.py:372
  199.5 11.5 %collective-permute-start.24 = (f16[64,1024]{1,0:T(8,128)(2,1)S(1)}, f16[64,1024]{1,0:T(8,128)(2,1)S(1)}, u32[]{:S(2)}, u32[]{:S(2)}) collective-permute-start(f16[64,1024]{1,0:T(8,128)(2,1)S(1)} %fusion.144), channel_id=1, source_target_pairs={{0,2},{1,3},{2,6},{3,7},{4,0},{5,1},{6,10},{7,11},{8,4},{9,5},{10,... | collective-permute-start | bytes 393224 | tf_op jit(solution)/shard_map/ppermute | solution.py:372
  202.2 5.0 %copy-start.27 = (f32[512]{0:T(512)S(1)}, f32[512]{0:T(512)}, u32[]{:S(2)}) copy-start(f32[512]{0:T(512)} %param.29) | copy-start | bytes 6148
  212.0 8.1 %collective-permute-start.27 = (f16[64,1024]{1,0:T(8,128)(2,1)S(1)}, f16[64,1024]{1,0:T(8,128)(2,1)}, u32[]{:S(2)}, u32[]{:S(2)}) collective-permute-start(f16[64,1024]{1,0:T(8,128)(2,1)S(1)} %fusion.143), channel_id=1, source_target_pairs={{0,4},{1,5},{2,0},{3,1},{4,8},{5,9},{6,2},{7,3},{8,12},{9,13},{10,... | collective-permute-start | bytes 393224 | tf_op jit(solution)/shard_map/ppermute | solution.py:372
  212.1 10.1 %collective-permute-start.28 = (f16[64,1024]{1,0:T(8,128)(2,1)S(1)}, f16[64,1024]{1,0:T(8,128)(2,1)}, u32[]{:S(2)}, u32[]{:S(2)}) collective-permute-start(f16[64,1024]{1,0:T(8,128)(2,1)S(1)} %fusion.142), channel_id=1, source_target_pairs={{0,2},{1,3},{2,6},{3,7},{4,0},{5,1},{6,10},{7,11},{8,4},{9,5},{10,... | collective-permute-start | bytes 393224 | tf_op jit(solution)/shard_map/ppermute | solution.py:372
  214.1 7.1 %collective-permute-start.29 = (f16[64,1024]{1,0:T(8,128)(2,1)}, f16[64,1024]{1,0:T(8,128)(2,1)}, u32[]{:S(2)}, u32[]{:S(2)}) collective-permute-start(f16[64,1024]{1,0:T(8,128)(2,1)} %fusion.141), channel_id=1, source_target_pairs={{0,4},{1,5},{2,0},{3,1},{4,8},{5,9},{6,2},{7,3},{8,12},{9,13},{10,... | collective-permute-start | bytes 393224 | tf_op jit(solution)/shard_map/ppermute | solution.py:372
  214.2 9.1 %collective-permute-start.30 = (f16[64,1024]{1,0:T(8,128)(2,1)S(1)}, f16[64,1024]{1,0:T(8,128)(2,1)}, u32[]{:S(2)}, u32[]{:S(2)}) collective-permute-start(f16[64,1024]{1,0:T(8,128)(2,1)S(1)} %fusion.140), channel_id=1, source_target_pairs={{0,2},{1,3},{2,6},{3,7},{4,0},{5,1},{6,10},{7,11},{8,4},{9,5},{10,... | collective-permute-start | bytes 393224 | tf_op jit(solution)/shard_map/ppermute | solution.py:372
  224.3 5.0 %collective-permute-start.31 = (f16[64,1024]{1,0:T(8,128)(2,1)S(1)}, f16[64,1024]{1,0:T(8,128)(2,1)S(1)}, u32[]{:S(2)}, u32[]{:S(2)}) collective-permute-start(f16[64,1024]{1,0:T(8,128)(2,1)S(1)} %fusion.139), channel_id=1, source_target_pairs={{0,4},{1,5},{2,0},{3,1},{4,8},{5,9},{6,2},{7,3},{8,12},{9,13},{10,... | collective-permute-start | bytes 393224 | tf_op jit(solution)/shard_map/ppermute | solution.py:372
  224.5 7.9 %collective-permute-start.32 = (f16[64,1024]{1,0:T(8,128)(2,1)S(1)}, f16[64,1024]{1,0:T(8,128)(2,1)S(1)}, u32[]{:S(2)}, u32[]{:S(2)}) collective-permute-start(f16[64,1024]{1,0:T(8,128)(2,1)S(1)} %fusion.138), channel_id=1, source_target_pairs={{0,2},{1,3},{2,6},{3,7},{4,0},{5,1},{6,10},{7,11},{8,4},{9,5},{10,... | collective-permute-start | bytes 393224 | tf_op jit(solution)/shard_map/ppermute | solution.py:372
  226.4 5.0 %collective-permute-start.33 = (f16[64,1024]{1,0:T(8,128)(2,1)S(1)}, f16[64,1024]{1,0:T(8,128)(2,1)S(1)}, u32[]{:S(2)}, u32[]{:S(2)}) collective-permute-start(f16[64,1024]{1,0:T(8,128)(2,1)S(1)} %fusion.137), channel_id=1, source_target_pairs={{0,4},{1,5},{2,0},{3,1},{4,8},{5,9},{6,2},{7,3},{8,12},{9,13},{10,... | collective-permute-start | bytes 393224 | tf_op jit(solution)/shard_map/ppermute | solution.py:372
  226.5 6.8 %collective-permute-start.34 = (f16[64,1024]{1,0:T(8,128)(2,1)S(1)}, f16[64,1024]{1,0:T(8,128)(2,1)S(1)}, u32[]{:S(2)}, u32[]{:S(2)}) collective-permute-start(f16[64,1024]{1,0:T(8,128)(2,1)S(1)} %fusion.136), channel_id=1, source_target_pairs={{0,2},{1,3},{2,6},{3,7},{4,0},{5,1},{6,10},{7,11},{8,4},{9,5},{10,... | collective-permute-start | bytes 393224 | tf_op jit(solution)/shard_map/ppermute | solution.py:372
  234.4 5.0 %collective-permute-start.38 = (f16[64,1024]{1,0:T(8,128)(2,1)S(1)}, f16[64,1024]{1,0:T(8,128)(2,1)S(1)}, u32[]{:S(2)}, u32[]{:S(2)}) collective-permute-start(f16[64,1024]{1,0:T(8,128)(2,1)S(1)} %fusion.132), channel_id=1, source_target_pairs={{0,2},{1,3},{2,6},{3,7},{4,0},{5,1},{6,10},{7,11},{8,4},{9,5},{10,... | collective-permute-start | bytes 393224 | tf_op jit(solution)/shard_map/ppermute | solution.py:372
  234.5 7.9 %collective-permute-start.37 = (f16[64,1024]{1,0:T(8,128)(2,1)S(1)}, f16[64,1024]{1,0:T(8,128)(2,1)S(1)}, u32[]{:S(2)}, u32[]{:S(2)}) collective-permute-start(f16[64,1024]{1,0:T(8,128)(2,1)S(1)} %fusion.133), channel_id=1, source_target_pairs={{0,4},{1,5},{2,0},{3,1},{4,8},{5,9},{6,2},{7,3},{8,12},{9,13},{10,... | collective-permute-start | bytes 393224 | tf_op jit(solution)/shard_map/ppermute | solution.py:372
  236.5 5.0 %collective-permute-start.36 = (f16[64,1024]{1,0:T(8,128)(2,1)S(1)}, f16[64,1024]{1,0:T(8,128)(2,1)S(1)}, u32[]{:S(2)}, u32[]{:S(2)}) collective-permute-start(f16[64,1024]{1,0:T(8,128)(2,1)S(1)} %fusion.134), channel_id=1, source_target_pairs={{0,2},{1,3},{2,6},{3,7},{4,0},{5,1},{6,10},{7,11},{8,4},{9,5},{10,... | collective-permute-start | bytes 393224 | tf_op jit(solution)/shard_map/ppermute | solution.py:372
  236.6 6.8 %collective-permute-start.35 = (f16[64,1024]{1,0:T(8,128)(2,1)S(1)}, f16[64,1024]{1,0:T(8,128)(2,1)S(1)}, u32[]{:S(2)}, u32[]{:S(2)}) collective-permute-start(f16[64,1024]{1,0:T(8,128)(2,1)S(1)} %fusion.135), channel_id=1, source_target_pairs={{0,4},{1,5},{2,0},{3,1},{4,8},{5,9},{6,2},{7,3},{8,12},{9,13},{10,... | collective-permute-start | bytes 393224 | tf_op jit(solution)/shard_map/ppermute | solution.py:372
  (3 other events, 4.1 us)

commit v3 on v2

--- a/solution.py
+++ b/solution.py
@@ -378,7 +378,7 @@
     moving = [ring.first() for ring in rings]
     steps = rings[0].chips - 1
     for step in range(max(steps, len(stages))):
-        moving, value = lax.optimization_barrier((moving, value))
+        value = lax.optimization_barrier((moving, value))[1]
         if step < steps:
             moving = [ring.step(block, step) for ring, block in zip(rings, moving)]
         if step < len(stages):

time: 247 us -> 247 us (level)
  waiting for transfers between devices: 9.25 us -> 2.6 us
    ppermute x28, waiting for transfers between devices: 7.51 us -> 0.96 us  [step(): moving = lax.ppermute(moving, 'lon', self.route).astype(jnp.float32)]
  transfers between devices with their start and end apart: 39 -> 39, of which waited for: 9 -> 2; matrix products, arithmetic and copies ran while one was open for 22% -> 26% of each run, Pallas kernels for 7% -> 7%
where the time goes in v3:
time: 247 us; the launch traced here: 246 us
  Pallas kernels  98 us (40%)
  other arithmetic  51 us (21%)
  starting transfers between devices  38.4 us (16%)
  matrix products  29.8 us (12%)
  local copies, waits for them, and re-layouts  20.1 us (8%)
  between operations  5.58 us (2%)
  waiting for transfers between devices  2.6 us (1%)
    pallas_call x1, Pallas kernels, gather_weights(): pl.pallas_call(functools.partial(gather_weights_kernel, n), out_shape=(ja...  66.4 us
    ppermute x28, starting transfers between devices, step(): moving = lax.ppermute(moving, 'lon', self.route).astype(jnp.float32)  29.2 us
    convert_element_type x24, other arithmetic, step(): moving.astype(jnp.float16)  28.3 us
    dot_general x12, matrix products, dot32(): return jnp.dot(left, right, preferred_element_type=jnp.float32)  25 us
    pallas_call x2, Pallas kernels, small_gather(): pl.pallas_call(functools.partial(small_gather_kernel, n), out_shape=jax.S...  16.1 us
    pallas_call x1, Pallas kernels, attention(): pl.pallas_call(attention_kernel, grid=(tokens // cells,), out_shape=(jax....  15.4 us
  transfers between devices with their start and end apart: 39, of which 2 were waited for; matrix products, arithmetic and copies ran while one was open for 26% of the time, Pallas kernels for 7%

profile of v3, /device:TPU:0, one launch (start us, length us, event | category | flops | bytes accessed | tf_op | source)
XLA Modules:
  0.0 245.5 jit_solution(7580614604754174871)
XLA Ops:
  0.7 1.0 fusion.166
  2.4 1.1 fusion.188
  4.2 66.4 %shard_map.184 = (bf16[1024,4096]{1,0:T(8,128)(2,1)}, f32[16,8,256]{2,1,0:T(8,128)}) custom-call(bf16[64,3072]{1,0:T(8,128)(2,1)} %proj_ref.1, bf16[64,1024]{1,0:T(8,128)(2,1)} %out_weight_ref.1, f32[8,256]{1,0:T(8,128)} %broadcast_in_dim.45.surface_ref), custom_call_target="tpu_custom_call" | custom-call | tf_op jit(solution)/shard_map/pallas_call | solution.py:230
  72.2 1.2 fusion.157
  73.4 1.2 add_convert_fusion
  74.7 2.5 %collective-permute-start = (bf16[8,4,1024]{2,1,0:T(4,128)(2,1)S(1)}, bf16[8,4,1024]{2,1,0:T(4,128)(2,1)S(1)}, u32[]{:S(2)}, u32[]{:S(2)}) collective-permute-start(bf16[8,4,1024]{2,1,0:T(4,128)(2,1)S(1)} %slice.462), channel_id=1, source_target_pairs={{1,0},{2,1},{3,2},{4,3},{5,4},{6,5},{7,6},{8,7},{9,8},{10,9},{11,1... | collective-permute-start | bytes 196616 | tf_op jit(solution)/shard_map/ppermute | solution.py:25
  79.8 1.2 slice.350
  84.0 4.8 %fusion.2.packed_ref = bf16[256,3072]{1,0:T(8,128)(2,1)S(1)} fusion(bf16[256,1024]{1,0:T(8,128)(2,1)S(1)} %multiply_convert_fusion, bf16[1024,4096]{1,0:T(8,128)(2,1)} %get-tuple-element.21), kind=kOutput, calls=%fused_computation.45 | convolution fusion | flops 1611399168 | bytes 8388608 | tf_op jit(solution)/shard_map/dot_general | solution.py:342
  88.7 2.5 %fusion.20.grad_ref = bf16[256,1024]{1,0:T(8,128)(2,1)S(1)} fusion(bf16[256,1024]{1,0:T(8,128)(2,1)} %bitcast.17, bf16[1024,4096]{1,0:T(8,128)(2,1)} %get-tuple-element.21), kind=kOutput, calls=%fused_computation.67 | convolution fusion | flops 537133056 | bytes 3145728 | tf_op jit(solution)/shard_map/dot_general | solution.py:439
  91.3 15.4 %shard_map.185 = (bf16[256,1024]{1,0:T(8,128)(2,1)S(1)}, bf16[256,3072]{1,0:T(8,128)(2,1)S(1)}) custom-call(bf16[256,3072]{1,0:T(8,128)(2,1)S(1)} %fusion.2.packed_ref, bf16[256,1024]{1,0:T(8,128)(2,1)S(1)} %fusion.20.grad_ref), custom_call_target="tpu_custom_call" | custom-call | flops 939524096 | bytes 4194304 | tf_op jit(solution)/shard_map/pallas_call | solution.py:312
  106.7 1.0 abs_reduce_fusion
  107.7 1.2 fusion.181
  110.6 2.0 copy.37
  112.6 2.2 constant_dynamic-slice_fusion
  114.8 1.8 fusion.177
  116.6 1.9 fusion.175
  122.7 8.0 %shard_map.186 = f32[16,8,128]{2,1,0:T(8,128)} custom-call(f32[8,128]{1,0:T(8,128)} %broadcast_in_dim.47.x_ref), custom_call_target="tpu_custom_call" | custom-call | tf_op jit(solution)/shard_map/pallas_call | solution.py:115
  130.7 1.5 slice_reduce_fusion
  133.9 1.5 fusion.173
  135.4 1.7 fusion.189
  137.3 1.6 convolution_add_fusion.3
  138.9 1.9 convolution_add_fusion.2
  140.8 1.9 convolution_add_fusion.1
  144.2 1.5 convolution_add_fusion
  145.8 1.3 copy-done.6
  147.7 2.3 fusion.23
  152.2 1.3 collective-permute-start.11
  154.3 1.3 collective-permute-start.26
  155.6 1.6 collective-permute-done.32
  158.9 1.2 fusion.155
  160.1 1.6 fusion.149
  161.8 2.0 collective-permute-start.12
  163.8 1.6 fusion.143
  165.5 1.6 fusion.137
  167.1 2.0 collective-permute-start.27
  171.3 1.0 fusion.148
  172.3 2.0 collective-permute-start.13
  174.4 1.7 fusion.142
  176.1 1.0 fusion.136
  177.1 2.0 collective-permute-start.28
  179.2 8.2 %shard_map.187 = f32[16,8,256]{2,1,0:T(8,128)} custom-call(f32[8,256]{1,0:T(8,128)} %reshape.270.x_ref), custom_call_target="tpu_custom_call" | custom-call | tf_op jit(solution)/shard_map/pallas_call | solution.py:115
  189.5 1.0 fusion.153
  190.5 1.0 fusion.141
  191.6 1.0 fusion.147
  192.6 1.0 fusion.135
  193.7 4.4 %collective-permute-start.34 = (bf16[8,3,512]{2,1,0:T(4,128)(2,1)S(1)}, bf16[8,3,512]{2,1,0:T(4,128)(2,1)S(1)}, u32[]{:S(2)}, u32[]{:S(2)}) collective-permute-start(bf16[8,3,512]{2,1,0:T(4,128)(2,1)S(1)} %get-tuple-element.49), channel_id=1, source_target_pairs={{1,0},{2,1},{3,2},{4,3},{5,4},{6,5},{7,6},{8,7},{9,8},{10,9},{11,1... | collective-permute-start | bytes 73736 | tf_op jit(solution)/shard_map/ppermute | solution.py:36
  200.1 2.0 collective-permute-start.14
  202.1 2.0 collective-permute-start.29
  204.6 4.5 %fusion.179 = (f32[8,32]{1,0:T(8,128)S(1)}, f32[8,32,512]{2,1,0:T(8,128)S(1)}) fusion(f32[512]{0:T(512)S(1)} %bitcast.366, f32[512]{0:T(512)S(1)} %bitcast.367, f32[512]{0:T(512)S(1)} %bitcast.320, f32[512]{0:T(512)S(1)} %bitcast.321, f32[512]{0:T(512)S(1)} %bitcast.322, f32[512]{0:T(512)S(1)} %bitcast.323, f32[512]{0:T(512)S(1)} %bitcast.324, ...), kind=kLoop, calls=%fused_computation.295 | loop fusion | flops 12844800 | bytes 4951040 | tf_op jit(solution)/shard_map/reduce_sum | solution.py:42
  211.6 2.1 collective-permute-start.15
  213.6 1.6 fusion.140
  215.3 1.6 fusion.134
  216.9 2.0 collective-permute-start.30
  218.9 3.2 %fusion.33 = f32[256,512]{1,0:T(8,128)S(1)} fusion(bf16[2048,512]{1,0:T(8,128)(2,1)S(1)} %copy-done, bf16[256,512]{1,0:T(8,128)(2,1)S(1)} %bitcast.314, bf16[512,2048]{1,0:T(8,128)(2,1)} %param.30), kind=kOutput, calls=%fused_computation.82 | convolution fusion | flops 1078460416 | bytes 4980736 | tf_op jit(solution)/shard_map/dot_general | solution.py:342
  224.0 1.0 fusion.145
  225.1 2.0 collective-permute-start.16
  227.1 1.0 fusion.139
  228.2 1.0 fusion.133
  229.2 2.0 collective-permute-start.31
  233.4 2.0 collective-permute-start.36
  237.5 2.0 collective-permute-start.38
  242.5 1.0 fusion.130
  243.5 1.0 fusion.128
  244.5 1.0 pad_maximum_fusion
  (242 shorter events, 37.2 us)
Async XLA Ops:
  0.6 218.3 %copy-start = (bf16[2048,512]{1,0:T(8,128)(2,1)S(1)}, bf16[2048,512]{1,0:T(8,128)(2,1)}, u32[]{:S(2)}) copy-start(bf16[2048,512]{1,0:T(8,128)(2,1)} %param.31) | copy-start | bytes 6291460
  0.6 77.6 %copy-start.16 = (f32[7,7,512]{2,1,0:T(8,128)S(1)}, f32[7,7,512]{2,1,0:T(8,128)}, u32[]{:S(2)}) copy-start(f32[7,7,512]{2,1,0:T(8,128)} %param.28) | copy-start | bytes 301060
  74.7 6.4 %collective-permute-start = (bf16[8,4,1024]{2,1,0:T(4,128)(2,1)S(1)}, bf16[8,4,1024]{2,1,0:T(4,128)(2,1)S(1)}, u32[]{:S(2)}, u32[]{:S(2)}) collective-permute-start(bf16[8,4,1024]{2,1,0:T(4,128)(2,1)S(1)} %slice.462), channel_id=1, source_target_pairs={{1,0},{2,1},{3,2},{4,3},{5,4},{6,5},{7,6},{8,7},{9,8},{10,9},{11,1... | collective-permute-start | bytes 196616 | tf_op jit(solution)/shard_map/ppermute | solution.py:25
  78.1 3.9 %collective-permute-start.1 = (bf16[8,4,1024]{2,1,0:T(4,128)(2,1)S(1)}, bf16[8,4,1024]{2,1,0:T(4,128)(2,1)S(1)}, u32[]{:S(2)}, u32[]{:S(2)}) collective-permute-start(bf16[8,4,1024]{2,1,0:T(4,128)(2,1)S(1)} %slice.351), channel_id=1, source_target_pairs={{1,0},{2,1},{3,2},{4,3},{5,4},{6,5},{7,6},{8,7},{9,8},{10,9},{11,1... | collective-permute-start | bytes 196616 | tf_op jit(solution)/shard_map/ppermute | solution.py:25
  118.4 25.8 %collective-permute-start.25 = (bf16[256,1024]{1,0:T(8,128)(2,1)}, bf16[256,1024]{1,0:T(8,128)(2,1)}, u32[]{:S(2)}, u32[]{:S(2)}) collective-permute-start(bf16[256,1024]{1,0:T(8,128)(2,1)} %bitcast.17), channel_id=1, source_target_pairs={{0,1},{1,0},{2,3},{3,2},{4,5},{5,4},{6,7},{7,6},{8,9},{9,8},{10,11... | collective-permute-start | bytes 1572872 | tf_op jit(solution)/shard_map/ppermute | solution.py:465
  132.2 4.9 %collective-permute-start.2 = (bf16[512,256]{1,0:T(8,128)(2,1)}, bf16[512,256]{1,0:T(8,128)(2,1)S(1)}, u32[]{:S(2)}, u32[]{:S(2)}) collective-permute-start(bf16[512,256]{1,0:T(8,128)(2,1)} %bitcast.316), channel_id=1, source_target_pairs={{0,1},{1,0},{2,3},{3,2},{4,5},{5,4},{6,7},{7,6},{8,9},{9,8},{10,11... | collective-permute-start | bytes 786440 | tf_op jit(solution)/shard_map/ppermute | solution.py:457
  132.3 5.0 %collective-permute-start.3 = (bf16[256,1024]{1,0:T(8,128)(2,1)}, bf16[256,1024]{1,0:T(8,128)(2,1)}, u32[]{:S(2)}, u32[]{:S(2)}) collective-permute-start(bf16[256,1024]{1,0:T(8,128)(2,1)} %get-tuple-element.43), channel_id=1, source_target_pairs={{0,1},{1,0},{2,3},{3,2},{4,5},{5,4},{6,7},{7,6},{8,9},{9,8},{10,11... | collective-permute-start | bytes 1572872 | tf_op jit(solution)/shard_map/ppermute | solution.py:465
  132.7 6.2 %collective-permute-start.10 = (bf16[256,1024]{1,0:T(8,128)(2,1)}, bf16[256,1024]{1,0:T(8,128)(2,1)}, u32[]{:S(2)}, u32[]{:S(2)}) collective-permute-start(bf16[256,1024]{1,0:T(8,128)(2,1)} %get-tuple-element.42), channel_id=1, source_target_pairs={{0,1},{1,0},{2,3},{3,2},{4,5},{5,4},{6,7},{7,6},{8,9},{9,8},{10,11... | collective-permute-start | bytes 1572872 | tf_op jit(solution)/shard_map/ppermute | solution.py:465
  132.8 8.0 %collective-permute-start.17 = (bf16[256,1024]{1,0:T(8,128)(2,1)}, bf16[256,1024]{1,0:T(8,128)(2,1)}, u32[]{:S(2)}, u32[]{:S(2)}) collective-permute-start(bf16[256,1024]{1,0:T(8,128)(2,1)} %get-tuple-element.41), channel_id=1, source_target_pairs={{0,1},{1,0},{2,3},{3,2},{4,5},{5,4},{6,7},{7,6},{8,9},{9,8},{10,11... | collective-permute-start | bytes 1572872 | tf_op jit(solution)/shard_map/ppermute | solution.py:465
  137.1 7.1 %collective-permute-start.24 = (bf16[512,256]{1,0:T(8,128)(2,1)S(1)}, bf16[512,256]{1,0:T(8,128)(2,1)S(1)}, u32[]{:S(2)}, u32[]{:S(2)}) collective-permute-start(bf16[512,256]{1,0:T(8,128)(2,1)S(1)} %bitcast.315), channel_id=1, source_target_pairs={{0,1},{1,0},{2,3},{3,2},{4,5},{5,4},{6,7},{7,6},{8,9},{9,8},{10,11... | collective-permute-start | bytes 786440 | tf_op jit(solution)/shard_map/ppermute | solution.py:457
  150.1 19.0 %copy-start.14 = (bf16[1,2,256,256]{3,2,1,0:T(8,128)(2,1)S(1)}, bf16[1,2,256,256]{3,2,1,0:T(8,128)(2,1)}, u32[]{:S(2)}) copy-start(bf16[1,2,256,256]{3,2,1,0:T(8,128)(2,1)} %param.32) | copy-start | bytes 786436
  150.1 19.0 %copy-start.19 = (bf16[1024,4]{0,1:T(4,128)(2,1)S(1)}, bf16[1024,4]{0,1:T(4,128)(2,1)}, u32[]{:S(2)}) copy-start(bf16[1024,4]{0,1:T(4,128)(2,1)} %param.26) | copy-start | bytes 24580
  150.2 7.0 %collective-permute-start.32 = (bf16[8,4,1024]{2,1,0:T(4,128)(2,1)S(1)}, bf16[8,4,1024]{2,1,0:T(4,128)(2,1)S(1)}, u32[]{:S(2)}, u32[]{:S(2)}) collective-permute-start(bf16[8,4,1024]{2,1,0:T(4,128)(2,1)S(1)} %slice.463), channel_id=1, source_target_pairs={{15,0},{0,1},{1,2},{2,3},{3,4},{4,5},{5,6},{6,7},{7,8},{8,9},{9,10... | collective-permute-start | bytes 196616 | tf_op jit(solution)/shard_map/ppermute | solution.py:25
  150.7 8.2 %collective-permute-start.4 = (f16[64,1024]{1,0:T(8,128)(2,1)}, f16[64,1024]{1,0:T(8,128)(2,1)}, u32[]{:S(2)}, u32[]{:S(2)}) collective-permute-start(f16[64,1024]{1,0:T(8,128)(2,1)} %fusion.159), channel_id=1, source_target_pairs={{0,4},{1,5},{2,0},{3,1},{4,8},{5,9},{6,2},{7,3},{8,12},{9,13},{10,... | collective-permute-start | bytes 393224 | tf_op jit(solution)/shard_map/ppermute | solution.py:372
  152.2 7.9 %collective-permute-start.11 = (f16[64,1024]{1,0:T(8,128)(2,1)}, f16[64,1024]{1,0:T(8,128)(2,1)S(1)}, u32[]{:S(2)}, u32[]{:S(2)}) collective-permute-start(f16[64,1024]{1,0:T(8,128)(2,1)} %fusion.160), channel_id=1, source_target_pairs={{0,2},{1,3},{2,6},{3,7},{4,0},{5,1},{6,10},{7,11},{8,4},{9,5},{10,... | collective-permute-start | bytes 393224 | tf_op jit(solution)/shard_map/ppermute | solution.py:372
  153.5 10.2 %collective-permute-start.18 = (f16[64,1024]{1,0:T(8,128)(2,1)S(1)}, f16[64,1024]{1,0:T(8,128)(2,1)S(1)}, u32[]{:S(2)}, u32[]{:S(2)}) collective-permute-start(f16[64,1024]{1,0:T(8,128)(2,1)S(1)} %fusion.161), channel_id=1, source_target_pairs={{0,4},{1,5},{2,0},{3,1},{4,8},{5,9},{6,2},{7,3},{8,12},{9,13},{10,... | collective-permute-start | bytes 393224 | tf_op jit(solution)/shard_map/ppermute | solution.py:372
  154.3 11.2 %collective-permute-start.26 = (f16[64,1024]{1,0:T(8,128)(2,1)}, f16[64,1024]{1,0:T(8,128)(2,1)S(1)}, u32[]{:S(2)}, u32[]{:S(2)}) collective-permute-start(f16[64,1024]{1,0:T(8,128)(2,1)} %fusion.162), channel_id=1, source_target_pairs={{0,2},{1,3},{2,6},{3,7},{4,0},{5,1},{6,10},{7,11},{8,4},{9,5},{10,... | collective-permute-start | bytes 393224 | tf_op jit(solution)/shard_map/ppermute | solution.py:372
  158.8 17.2 %copy-start.10 = (bf16[8,32,1024]{2,1,0:T(8,128)(2,1)}, bf16[8,32,1024]{2,1,0:T(8,128)(2,1)S(1)}, u32[]{:S(2)}) copy-start(bf16[8,32,1024]{2,1,0:T(8,128)(2,1)S(1)} %pad_maximum_fusion.1) | copy-start | bytes 1572868
  160.1 10.1 %collective-permute-start.5 = (f16[64,1024]{1,0:T(8,128)(2,1)S(1)}, f16[64,1024]{1,0:T(8,128)(2,1)S(1)}, u32[]{:S(2)}, u32[]{:S(2)}) collective-permute-start(f16[64,1024]{1,0:T(8,128)(2,1)S(1)} %fusion.155), channel_id=1, source_target_pairs={{0,4},{1,5},{2,0},{3,1},{4,8},{5,9},{6,2},{7,3},{8,12},{9,13},{10,... | collective-permute-start | bytes 393224 | tf_op jit(solution)/shard_map/ppermute | solution.py:372
  161.8 26.7 %copy-start.9 = (bf16[8,32,512]{2,1,0:T(8,128)(2,1)S(1)}, bf16[8,32,512]{2,1,0:T(8,128)(2,1)}, u32[]{:S(2)}) copy-start(bf16[8,32,512]{2,1,0:T(8,128)(2,1)} %param.19) | copy-start | bytes 786436
  161.8 26.7 %copy-start.20 = (f32[4,512]{1,0:T(4,128)S(1)}, f32[4,512]{1,0:T(4,128)}, u32[]{:S(2)}) copy-start(f32[4,512]{1,0:T(4,128)} %param.27) | copy-start | bytes 24580
  161.8 9.5 %collective-permute-start.12 = (f16[64,1024]{1,0:T(8,128)(2,1)}, f16[64,1024]{1,0:T(8,128)(2,1)}, u32[]{:S(2)}, u32[]{:S(2)}) collective-permute-start(f16[64,1024]{1,0:T(8,128)(2,1)} %fusion.149), channel_id=1, source_target_pairs={{0,2},{1,3},{2,6},{3,7},{4,0},{5,1},{6,10},{7,11},{8,4},{9,5},{10,... | collective-permute-start | bytes 393224 | tf_op jit(solution)/shard_map/ppermute | solution.py:372
  165.4 8.9 %collective-permute-start.19 = (f16[64,1024]{1,0:T(8,128)(2,1)}, f16[64,1024]{1,0:T(8,128)(2,1)}, u32[]{:S(2)}, u32[]{:S(2)}) collective-permute-start(f16[64,1024]{1,0:T(8,128)(2,1)} %fusion.143), channel_id=1, source_target_pairs={{0,4},{1,5},{2,0},{3,1},{4,8},{5,9},{6,2},{7,3},{8,12},{9,13},{10,... | collective-permute-start | bytes 393224 | tf_op jit(solution)/shard_map/ppermute | solution.py:372
  167.1 9.0 %collective-permute-start.27 = (f16[64,1024]{1,0:T(8,128)(2,1)}, f16[64,1024]{1,0:T(8,128)(2,1)}, u32[]{:S(2)}, u32[]{:S(2)}) collective-permute-start(f16[64,1024]{1,0:T(8,128)(2,1)} %fusion.137), channel_id=1, source_target_pairs={{0,2},{1,3},{2,6},{3,7},{4,0},{5,1},{6,10},{7,11},{8,4},{9,5},{10,... | collective-permute-start | bytes 393224 | tf_op jit(solution)/shard_map/ppermute | solution.py:372
  171.2 18.3 %collective-permute-start.6 = (f16[64,1024]{1,0:T(8,128)(2,1)S(1)}, f16[64,1024]{1,0:T(8,128)(2,1)}, u32[]{:S(2)}, u32[]{:S(2)}) collective-permute-start(f16[64,1024]{1,0:T(8,128)(2,1)S(1)} %fusion.154), channel_id=1, source_target_pairs={{0,4},{1,5},{2,0},{3,1},{4,8},{5,9},{6,2},{7,3},{8,12},{9,13},{10,... | collective-permute-start | bytes 393224 | tf_op jit(solution)/shard_map/ppermute | solution.py:372
  172.3 19.2 %collective-permute-start.13 = (f16[64,1024]{1,0:T(8,128)(2,1)S(1)}, f16[64,1024]{1,0:T(8,128)(2,1)S(1)}, u32[]{:S(2)}, u32[]{:S(2)}) collective-permute-start(f16[64,1024]{1,0:T(8,128)(2,1)S(1)} %fusion.148), channel_id=1, source_target_pairs={{0,2},{1,3},{2,6},{3,7},{4,0},{5,1},{6,10},{7,11},{8,4},{9,5},{10,... | collective-permute-start | bytes 393224 | tf_op jit(solution)/shard_map/ppermute | solution.py:372
  176.0 14.5 %collective-permute-start.20 = (f16[64,1024]{1,0:T(8,128)(2,1)}, f16[64,1024]{1,0:T(8,128)(2,1)}, u32[]{:S(2)}, u32[]{:S(2)}) collective-permute-start(f16[64,1024]{1,0:T(8,128)(2,1)} %fusion.142), channel_id=1, source_target_pairs={{0,4},{1,5},{2,0},{3,1},{4,8},{5,9},{6,2},{7,3},{8,12},{9,13},{10,... | collective-permute-start | bytes 393224 | tf_op jit(solution)/shard_map/ppermute | solution.py:372
  177.1 15.5 %collective-permute-start.28 = (f16[64,1024]{1,0:T(8,128)(2,1)S(1)}, f16[64,1024]{1,0:T(8,128)(2,1)S(1)}, u32[]{:S(2)}, u32[]{:S(2)}) collective-permute-start(f16[64,1024]{1,0:T(8,128)(2,1)S(1)} %fusion.136), channel_id=1, source_target_pairs={{0,2},{1,3},{2,6},{3,7},{4,0},{5,1},{6,10},{7,11},{8,4},{9,5},{10,... | collective-permute-start | bytes 393224 | tf_op jit(solution)/shard_map/ppermute | solution.py:372
  189.1 15.2 %copy-start.21 = (f32[1,1,512]{2,1,0:T(1,128)S(1)}, f32[1,1,512]{2,1,0:T(1,128)}, u32[]{:S(2)}) copy-start(f32[1,1,512]{2,1,0:T(1,128)} %get-tuple-element.50) | copy-start | bytes 6148
  189.1 15.2 %copy-start.22 = (f32[1,1,512]{2,1,0:T(1,128)S(1)}, f32[1,1,512]{2,1,0:T(1,128)}, u32[]{:S(2)}) copy-start(f32[1,1,512]{2,1,0:T(1,128)} %get-tuple-element.51) | copy-start | bytes 6148
  189.1 15.2 %copy-start.23 = (f32[1,1,512]{2,1,0:T(1,128)S(1)}, f32[1,1,512]{2,1,0:T(1,128)}, u32[]{:S(2)}) copy-start(f32[1,1,512]{2,1,0:T(1,128)} %get-tuple-element.52) | copy-start | bytes 6148
  189.1 15.2 %copy-start.24 = (f32[1,1,512]{2,1,0:T(1,128)S(1)}, f32[1,1,512]{2,1,0:T(1,128)}, u32[]{:S(2)}) copy-start(f32[1,1,512]{2,1,0:T(1,128)} %get-tuple-element.53) | copy-start | bytes 6148
  189.1 15.2 %copy-start.25 = (f32[1,1,512]{2,1,0:T(1,128)S(1)}, f32[1,1,512]{2,1,0:T(1,128)}, u32[]{:S(2)}) copy-start(f32[1,1,512]{2,1,0:T(1,128)} %get-tuple-element.54) | copy-start | bytes 6148
  189.2 15.2 %copy-start.26 = (f32[1,1,512]{2,1,0:T(1,128)S(1)}, f32[1,1,512]{2,1,0:T(1,128)}, u32[]{:S(2)}) copy-start(f32[1,1,512]{2,1,0:T(1,128)} %get-tuple-element.55) | copy-start | bytes 6148
  189.2 15.2 %copy-start.27 = (f32[1,1,512]{2,1,0:T(1,128)S(1)}, f32[1,1,512]{2,1,0:T(1,128)}, u32[]{:S(2)}) copy-start(f32[1,1,512]{2,1,0:T(1,128)} %get-tuple-element.56) | copy-start | bytes 6148
  189.2 15.2 %copy-start.28 = (f32[1,1,512]{2,1,0:T(1,128)S(1)}, f32[1,1,512]{2,1,0:T(1,128)}, u32[]{:S(2)}) copy-start(f32[1,1,512]{2,1,0:T(1,128)} %get-tuple-element.57) | copy-start | bytes 6148
  189.2 15.2 %copy-start.29 = (f32[1,1,512]{2,1,0:T(1,128)S(1)}, f32[1,1,512]{2,1,0:T(1,128)}, u32[]{:S(2)}) copy-start(f32[1,1,512]{2,1,0:T(1,128)} %get-tuple-element.58) | copy-start | bytes 6148
  189.2 15.2 %copy-start.30 = (f32[1,1,512]{2,1,0:T(1,128)S(1)}, f32[1,1,512]{2,1,0:T(1,128)}, u32[]{:S(2)}) copy-start(f32[1,1,512]{2,1,0:T(1,128)} %get-tuple-element.59) | copy-start | bytes 6148
  189.2 15.2 %copy-start.31 = (f32[1,1,512]{2,1,0:T(1,128)S(1)}, f32[1,1,512]{2,1,0:T(1,128)}, u32[]{:S(2)}) copy-start(f32[1,1,512]{2,1,0:T(1,128)} %get-tuple-element.60) | copy-start | bytes 6148
  189.2 15.2 %copy-start.32 = (f32[1,1,512]{2,1,0:T(1,128)S(1)}, f32[1,1,512]{2,1,0:T(1,128)}, u32[]{:S(2)}) copy-start(f32[1,1,512]{2,1,0:T(1,128)} %get-tuple-element.61) | copy-start | bytes 6148
  189.2 15.2 %copy-start.33 = (f32[1,1,512]{2,1,0:T(1,128)S(1)}, f32[1,1,512]{2,1,0:T(1,128)}, u32[]{:S(2)}) copy-start(f32[1,1,512]{2,1,0:T(1,128)} %get-tuple-element.62) | copy-start | bytes 6148
  189.2 15.2 %copy-start.34 = (f32[1,1,512]{2,1,0:T(1,128)S(1)}, f32[1,1,512]{2,1,0:T(1,128)}, u32[]{:S(2)}) copy-start(f32[1,1,512]{2,1,0:T(1,128)} %get-tuple-element.63) | copy-start | bytes 6148
  189.2 15.2 %copy-start.35 = (f32[1,1,512]{2,1,0:T(1,128)S(1)}, f32[1,1,512]{2,1,0:T(1,128)}, u32[]{:S(2)}) copy-start(f32[1,1,512]{2,1,0:T(1,128)} %get-tuple-element.64) | copy-start | bytes 6148
  189.3 15.2 %copy-start.36 = (f32[1,1,512]{2,1,0:T(1,128)S(1)}, f32[1,1,512]{2,1,0:T(1,128)}, u32[]{:S(2)}) copy-start(f32[1,1,512]{2,1,0:T(1,128)} %get-tuple-element.65) | copy-start | bytes 6148
  189.3 15.2 %copy-start.37 = (f32[1,1,512]{2,1,0:T(1,128)S(1)}, f32[1,1,512]{2,1,0:T(1,128)}, u32[]{:S(2)}) copy-start(f32[1,1,512]{2,1,0:T(1,128)} %get-tuple-element.66) | copy-start | bytes 6148
  189.3 15.2 %copy-start.38 = (f32[1,1,512]{2,1,0:T(1,128)S(1)}, f32[1,1,512]{2,1,0:T(1,128)}, u32[]{:S(2)}) copy-start(f32[1,1,512]{2,1,0:T(1,128)} %get-tuple-element.67) | copy-start | bytes 6148
  193.6 8.5 %collective-permute-start.33 = (bf16[8,3,512]{2,1,0:T(4,128)(2,1)S(1)}, bf16[8,3,512]{2,1,0:T(4,128)(2,1)S(1)}, u32[]{:S(2)}, u32[]{:S(2)}) collective-permute-start(bf16[8,3,512]{2,1,0:T(4,128)(2,1)S(1)} %get-tuple-element.48), channel_id=1, source_target_pairs={{0,1},{1,2},{2,3},{3,4},{4,5},{5,6},{6,7},{7,8},{8,9},{9,10},{10,1... | collective-permute-start | bytes 73736 | tf_op jit(solution)/shard_map/ppermute | solution.py:35
  193.7 10.5 %collective-permute-start.34 = (bf16[8,3,512]{2,1,0:T(4,128)(2,1)S(1)}, bf16[8,3,512]{2,1,0:T(4,128)(2,1)S(1)}, u32[]{:S(2)}, u32[]{:S(2)}) collective-permute-start(bf16[8,3,512]{2,1,0:T(4,128)(2,1)S(1)} %get-tuple-element.49), channel_id=1, source_target_pairs={{1,0},{2,1},{3,2},{4,3},{5,4},{6,5},{7,6},{8,7},{9,8},{10,9},{11,1... | collective-permute-start | bytes 73736 | tf_op jit(solution)/shard_map/ppermute | solution.py:36
  200.1 9.4 %collective-permute-start.7 = (f16[64,1024]{1,0:T(8,128)(2,1)S(1)}, f16[64,1024]{1,0:T(8,128)(2,1)S(1)}, u32[]{:S(2)}, u32[]{:S(2)}) collective-permute-start(f16[64,1024]{1,0:T(8,128)(2,1)S(1)} %fusion.153), channel_id=1, source_target_pairs={{0,4},{1,5},{2,0},{3,1},{4,8},{5,9},{6,2},{7,3},{8,12},{9,13},{10,... | collective-permute-start | bytes 393224 | tf_op jit(solution)/shard_map/ppermute | solution.py:372
  200.1 10.5 %collective-permute-start.14 = (f16[64,1024]{1,0:T(8,128)(2,1)S(1)}, f16[64,1024]{1,0:T(8,128)(2,1)S(1)}, u32[]{:S(2)}, u32[]{:S(2)}) collective-permute-start(f16[64,1024]{1,0:T(8,128)(2,1)S(1)} %fusion.147), channel_id=1, source_target_pairs={{0,2},{1,3},{2,6},{3,7},{4,0},{5,1},{6,10},{7,11},{8,4},{9,5},{10,... | collective-permute-start | bytes 393224 | tf_op jit(solution)/shard_map/ppermute | solution.py:372
  202.1 11.5 %collective-permute-start.21 = (f16[64,1024]{1,0:T(8,128)(2,1)S(1)}, f16[64,1024]{1,0:T(8,128)(2,1)S(1)}, u32[]{:S(2)}, u32[]{:S(2)}) collective-permute-start(f16[64,1024]{1,0:T(8,128)(2,1)S(1)} %fusion.141), channel_id=1, source_target_pairs={{0,4},{1,5},{2,0},{3,1},{4,8},{5,9},{6,2},{7,3},{8,12},{9,13},{10,... | collective-permute-start | bytes 393224 | tf_op jit(solution)/shard_map/ppermute | solution.py:372
  202.1 13.2 %collective-permute-start.29 = (f16[64,1024]{1,0:T(8,128)(2,1)S(1)}, f16[64,1024]{1,0:T(8,128)(2,1)S(1)}, u32[]{:S(2)}, u32[]{:S(2)}) collective-permute-start(f16[64,1024]{1,0:T(8,128)(2,1)S(1)} %fusion.135), channel_id=1, source_target_pairs={{0,2},{1,3},{2,6},{3,7},{4,0},{5,1},{6,10},{7,11},{8,4},{9,5},{10,... | collective-permute-start | bytes 393224 | tf_op jit(solution)/shard_map/ppermute | solution.py:372
  210.5 12.4 %collective-permute-start.8 = (f16[64,1024]{1,0:T(8,128)(2,1)S(1)}, f16[64,1024]{1,0:T(8,128)(2,1)S(1)}, u32[]{:S(2)}, u32[]{:S(2)}) collective-permute-start(f16[64,1024]{1,0:T(8,128)(2,1)S(1)} %fusion.152), channel_id=1, source_target_pairs={{0,4},{1,5},{2,0},{3,1},{4,8},{5,9},{6,2},{7,3},{8,12},{9,13},{10,... | collective-permute-start | bytes 393224 | tf_op jit(solution)/shard_map/ppermute | solution.py:372
  211.6 12.5 %collective-permute-start.15 = (f16[64,1024]{1,0:T(8,128)(2,1)S(1)}, f16[64,1024]{1,0:T(8,128)(2,1)}, u32[]{:S(2)}, u32[]{:S(2)}) collective-permute-start(f16[64,1024]{1,0:T(8,128)(2,1)S(1)} %fusion.146), channel_id=1, source_target_pairs={{0,2},{1,3},{2,6},{3,7},{4,0},{5,1},{6,10},{7,11},{8,4},{9,5},{10,... | collective-permute-start | bytes 393224 | tf_op jit(solution)/shard_map/ppermute | solution.py:372
  215.3 11.8 %collective-permute-start.22 = (f16[64,1024]{1,0:T(8,128)(2,1)}, f16[64,1024]{1,0:T(8,128)(2,1)}, u32[]{:S(2)}, u32[]{:S(2)}) collective-permute-start(f16[64,1024]{1,0:T(8,128)(2,1)} %fusion.140), channel_id=1, source_target_pairs={{0,4},{1,5},{2,0},{3,1},{4,8},{5,9},{6,2},{7,3},{8,12},{9,13},{10,... | collective-permute-start | bytes 393224 | tf_op jit(solution)/shard_map/ppermute | solution.py:372
  216.9 11.3 %collective-permute-start.30 = (f16[64,1024]{1,0:T(8,128)(2,1)}, f16[64,1024]{1,0:T(8,128)(2,1)}, u32[]{:S(2)}, u32[]{:S(2)}) collective-permute-start(f16[64,1024]{1,0:T(8,128)(2,1)} %fusion.134), channel_id=1, source_target_pairs={{0,2},{1,3},{2,6},{3,7},{4,0},{5,1},{6,10},{7,11},{8,4},{9,5},{10,... | collective-permute-start | bytes 393224 | tf_op jit(solution)/shard_map/ppermute | solution.py:372
  223.9 7.4 %collective-permute-start.9 = (f16[64,1024]{1,0:T(8,128)(2,1)S(1)}, f16[64,1024]{1,0:T(8,128)(2,1)S(1)}, u32[]{:S(2)}, u32[]{:S(2)}) collective-permute-start(f16[64,1024]{1,0:T(8,128)(2,1)S(1)} %fusion.151), channel_id=1, source_target_pairs={{0,4},{1,5},{2,0},{3,1},{4,8},{5,9},{6,2},{7,3},{8,12},{9,13},{10,... | collective-permute-start | bytes 393224 | tf_op jit(solution)/shard_map/ppermute | solution.py:372
  225.1 7.3 %collective-permute-start.16 = (f16[64,1024]{1,0:T(8,128)(2,1)S(1)}, f16[64,1024]{1,0:T(8,128)(2,1)S(1)}, u32[]{:S(2)}, u32[]{:S(2)}) collective-permute-start(f16[64,1024]{1,0:T(8,128)(2,1)S(1)} %fusion.145), channel_id=1, source_target_pairs={{0,2},{1,3},{2,6},{3,7},{4,0},{5,1},{6,10},{7,11},{8,4},{9,5},{10,... | collective-permute-start | bytes 393224 | tf_op jit(solution)/shard_map/ppermute | solution.py:372
  228.1 7.3 %collective-permute-start.23 = (f16[64,1024]{1,0:T(8,128)(2,1)S(1)}, f16[64,1024]{1,0:T(8,128)(2,1)S(1)}, u32[]{:S(2)}, u32[]{:S(2)}) collective-permute-start(f16[64,1024]{1,0:T(8,128)(2,1)S(1)} %fusion.139), channel_id=1, source_target_pairs={{0,4},{1,5},{2,0},{3,1},{4,8},{5,9},{6,2},{7,3},{8,12},{9,13},{10,... | collective-permute-start | bytes 393224 | tf_op jit(solution)/shard_map/ppermute | solution.py:372
  229.2 7.3 %collective-permute-start.31 = (f16[64,1024]{1,0:T(8,128)(2,1)S(1)}, f16[64,1024]{1,0:T(8,128)(2,1)S(1)}, u32[]{:S(2)}, u32[]{:S(2)}) collective-permute-start(f16[64,1024]{1,0:T(8,128)(2,1)S(1)} %fusion.133), channel_id=1, source_target_pairs={{0,2},{1,3},{2,6},{3,7},{4,0},{5,1},{6,10},{7,11},{8,4},{9,5},{10,... | collective-permute-start | bytes 393224 | tf_op jit(solution)/shard_map/ppermute | solution.py:372
  232.3 7.3 %collective-permute-start.35 = (f16[64,1024]{1,0:T(8,128)(2,1)S(1)}, f16[64,1024]{1,0:T(8,128)(2,1)S(1)}, u32[]{:S(2)}, u32[]{:S(2)}) collective-permute-start(f16[64,1024]{1,0:T(8,128)(2,1)S(1)} %fusion.150), channel_id=1, source_target_pairs={{0,4},{1,5},{2,0},{3,1},{4,8},{5,9},{6,2},{7,3},{8,12},{9,13},{10,... | collective-permute-start | bytes 393224 | tf_op jit(solution)/shard_map/ppermute | solution.py:372
  233.4 9.1 %collective-permute-start.36 = (f16[64,1024]{1,0:T(8,128)(2,1)S(1)}, f16[64,1024]{1,0:T(8,128)(2,1)S(1)}, u32[]{:S(2)}, u32[]{:S(2)}) collective-permute-start(f16[64,1024]{1,0:T(8,128)(2,1)S(1)} %fusion.144), channel_id=1, source_target_pairs={{0,2},{1,3},{2,6},{3,7},{4,0},{5,1},{6,10},{7,11},{8,4},{9,5},{10,... | collective-permute-start | bytes 393224 | tf_op jit(solution)/shard_map/ppermute | solution.py:372
  236.4 5.0 %collective-permute-start.37 = (f16[64,1024]{1,0:T(8,128)(2,1)S(1)}, f16[64,1024]{1,0:T(8,128)(2,1)S(1)}, u32[]{:S(2)}, u32[]{:S(2)}) collective-permute-start(f16[64,1024]{1,0:T(8,128)(2,1)S(1)} %fusion.138), channel_id=1, source_target_pairs={{0,4},{1,5},{2,0},{3,1},{4,8},{5,9},{6,2},{7,3},{8,12},{9,13},{10,... | collective-permute-start | bytes 393224 | tf_op jit(solution)/shard_map/ppermute | solution.py:372
  237.5 5.9 %collective-permute-start.38 = (f16[64,1024]{1,0:T(8,128)(2,1)S(1)}, f16[64,1024]{1,0:T(8,128)(2,1)S(1)}, u32[]{:S(2)}, u32[]{:S(2)}) collective-permute-start(f16[64,1024]{1,0:T(8,128)(2,1)S(1)} %fusion.132), channel_id=1, source_target_pairs={{0,2},{1,3},{2,6},{3,7},{4,0},{5,1},{6,10},{7,11},{8,4},{9,5},{10,... | collective-permute-start | bytes 393224 | tf_op jit(solution)/shard_map/ppermute | solution.py:372
  (33 other events, 298.9 us)
